TPU v7x, 32 devices: a whole 2x2x4 slice. The times are simulated.
32 devices in a mesh: wide: 16 (over z, x, core), narrow: 2 (over y).
Axes of the slice: x: 2, y: 2, z: 4, core: 2. Of those that a mesh axis runs over, the one named last changes fastest.
Arguments:
- inputs: bfloat16 [64, 256, 768], P(('wide', 'narrow')), may hold values from -6 to 6
- encoded: bfloat16 [64, 1024, 768], P(('wide', 'narrow')), may hold values from -6 to 6
- target_lengths: int32 [64], P(('wide', 'narrow')), may hold values from 32 to 256, as said below
- memory_lengths: int32 [64], P(('wide', 'narrow')), may hold values from 40 to 1024, as said below
- buckets: int32 [256, 256], replicated, may hold values from 0 to 31
- cotangent: bfloat16 [64, 256, 768], P(('wide', 'narrow')), may hold values from -6 to 6
- self_inward: bfloat16 [768, 2304], P('wide', 'narrow'), may hold values from -0.21875 to 0.21875
- self_outward: bfloat16 [768, 768], P('wide', 'narrow'), may hold values from -1.75 to 1.75
- cross_query: bfloat16 [768, 768], P('wide', 'narrow'), may hold values from -0.21875 to 0.21875
- cross_reader: bfloat16 [768, 1536], P('wide', 'narrow'), may hold values from -0.21875 to 0.21875
- cross_writer: bfloat16 [768, 768], P('wide', 'narrow'), may hold values from -3.5 to 3.5
- expand_weight: bfloat16 [768, 3072], P('wide', 'narrow'), may hold values from -0.21875 to 0.21875
- shrink_weight: bfloat16 [3072, 768], P('wide', 'narrow'), may hold values from -0.3125 to 0.3125
- norm_gains: float32 [3, 768], replicated, may hold values from 0.5 to 1.5
- bias_table: float32 [32, 12], replicated, may hold values from -5 to 5
Outputs:
- layer_out: bfloat16 [64, 256, 768], P(('wide', 'narrow'))
- inputs_grad: float32 [64, 256, 768], P(('wide', 'narrow'))
- encoded_grad: float32 [64, 1024, 768], P(('wide', 'narrow'))
- inward_grad: float32 [768, 2304], P('wide', 'narrow')
- inward_step: float32 [768, 2304], P('wide', 'narrow')
- inward_rows: float32 [768], P('wide')
- inward_cols: float32 [2304], P('narrow')
- outward_grad: float32 [768, 768], P('wide', 'narrow')
- outward_step: float32 [768, 768], P('wide', 'narrow')
- outward_rows: float32 [768], P('wide')
- outward_cols: float32 [768], P('narrow')
- query_grad: float32 [768, 768], P('wide', 'narrow')
- query_step: float32 [768, 768], P('wide', 'narrow')
- query_rows: float32 [768], P('wide')
- query_cols: float32 [768], P('narrow')
- reader_grad: float32 [768, 1536], P('wide', 'narrow')
- reader_step: float32 [768, 1536], P('wide', 'narrow')
- reader_rows: float32 [768], P('wide')
- reader_cols: float32 [1536], P('narrow')
- writer_grad: float32 [768, 768], P('wide', 'narrow')
- writer_step: float32 [768, 768], P('wide', 'narrow')
- writer_rows: float32 [768], P('wide')
- writer_cols: float32 [768], P('narrow')
- expand_grad: float32 [768, 3072], P('wide', 'narrow')
- expand_step: float32 [768, 3072], P('wide', 'narrow')
- expand_rows: float32 [768], P('wide')
- expand_cols: float32 [3072], P('narrow')
- shrink_grad: float32 [3072, 768], P('wide', 'narrow')
- shrink_step: float32 [3072, 768], P('wide', 'narrow')
- shrink_rows: float32 [3072], P('wide')
- shrink_cols: float32 [768], P('narrow')
- gains_grad: float32 [3, 768], replicated
- table_grad: float32 [32, 12], replicated
Inputs may be any that keep to these rules, and one draw needn't show every extreme that they name: `target_lengths`: some sequence has exactly 256 valid target positions and some exactly 32. `memory_lengths`: most sequences are short; some sequence has exactly 1024 valid memory positions and some exactly 40.
All inputs are finite; a program needn't handle non-finite values.
Results may differ from a plain program's by a relative error of at most 0.02.
Values may be sent and summed in bfloat16 or wider, within the bound.
No kernel may reach another device: no remote copies, remote signals or barrier semaphores. Data moves between devices by JAX's collectives and lax.ppermute only.
A program may use at most 192 MiB of HBM per device.

v0:
```python
import jax
import jax.numpy as jnp
from jax import lax
from jax.sharding import PartitionSpec as P

HEADS = 12
DH = 64


EPS = 1e-06
TINY = 1e-30
NEGATIVE = -1e30


def norm_row(values, gain):
    return values * lax.rsqrt(jnp.mean(values * values, axis=-1, keepdims=True) + EPS) * gain


def exact_gelu(values):
    return jax.nn.gelu(values, approximate=False)


def project(left, right):
    return jnp.einsum("std,de->ste", left, right, preferred_element_type=jnp.float32)


def project_back(grad, right):
    return jnp.einsum("ste,de->std", grad, right, preferred_element_type=jnp.float32)


def weight_grad(left, grad):
    return jnp.einsum("std,ste->de", left, grad, preferred_element_type=jnp.float32)


def split_heads(packed, count):
    seqs, length, width = packed.shape
    shaped = packed.reshape(seqs, length, count, HEADS, DH)
    moved = jnp.transpose(shaped, (2, 3, 0, 1, 4))
    return tuple((moved[index] for index in range(count)))


def merge_heads(pieces):
    heads, seqs, length, size = pieces.shape
    return jnp.transpose(pieces, (1, 2, 0, 3)).reshape(seqs, length, heads * size)


def head_scores(query, keys, extra, allowed):
    raw = (
        jnp.einsum("sqd,skd->sqk", query, keys, preferred_element_type=jnp.float32) * DH ** (-0.5)
        + extra
    )
    return jnp.where(allowed, raw, NEGATIVE)


def attend_forward(query, keys, values, extra, allowed):

    def one_head(pieces):
        head_query, head_keys, head_values, head_extra = pieces
        scores = head_scores(head_query, head_keys, head_extra, allowed)
        highest = jnp.max(scores, axis=-1, keepdims=True)
        weights = jnp.exp(scores - highest)
        totals = jnp.sum(weights, axis=-1, keepdims=True)
        probs = (weights / totals).astype(jnp.bfloat16)
        mixed = jnp.einsum("sqk,skd->sqd", probs, head_values, preferred_element_type=jnp.float32)
        return (mixed.astype(jnp.bfloat16), (highest + jnp.log(totals))[..., 0])

    mixed, logsum = lax.map(one_head, (query, keys, values, extra))
    return (merge_heads(mixed), logsum)


def attend_backward(query, keys, values, extra, allowed, logsum, grad_mixed, with_bias):

    def one_head(pieces):
        head_query, head_keys, head_values, head_extra, head_logsum, head_grad = pieces
        probs = jnp.exp(
            head_scores(head_query, head_keys, head_extra, allowed) - head_logsum[..., None]
        )
        grad_probs = jnp.einsum(
            "sqd,skd->sqk", head_grad, head_values, preferred_element_type=jnp.float32
        )
        grad_values = jnp.einsum(
            "sqk,sqd->skd",
            probs.astype(jnp.bfloat16),
            head_grad,
            preferred_element_type=jnp.float32,
        )
        inner = jnp.sum(probs * grad_probs, axis=-1, keepdims=True)
        grad_scores = (probs * (grad_probs - inner)).astype(jnp.bfloat16)
        grad_query = jnp.einsum(
            "sqk,skd->sqd", grad_scores, head_keys, preferred_element_type=jnp.float32
        ) * DH ** (-0.5)
        grad_keys = jnp.einsum(
            "sqk,sqd->skd", grad_scores, head_query, preferred_element_type=jnp.float32
        ) * DH ** (-0.5)
        if with_bias:
            grad_bias = jnp.sum(grad_scores, axis=0, dtype=jnp.float32)
        else:
            grad_bias = jnp.zeros((), jnp.float32)
        return (grad_query, grad_keys, grad_values, grad_bias)

    return lax.map(one_head, (query, keys, values, extra, logsum, grad_mixed))


def fetch(shards):
    first, second, third, fourth, fifth, sixth, seventh = shards
    first, second, third, fourth, fifth, sixth, seventh = (
        lax.all_gather(first, "narrow", axis=1, tiled=True),
        lax.all_gather(second, "narrow", axis=1, tiled=True),
        lax.all_gather(third, "narrow", axis=1, tiled=True),
        lax.all_gather(fourth, "narrow", axis=1, tiled=True),
        lax.all_gather(fifth, "narrow", axis=1, tiled=True),
        lax.all_gather(sixth, "narrow", axis=1, tiled=True),
        lax.all_gather(seventh, "narrow", axis=1, tiled=True),
    )
    return (
        lax.all_gather(first, "wide", axis=0, tiled=True),
        lax.all_gather(second, "wide", axis=0, tiled=True),
        lax.all_gather(third, "wide", axis=0, tiled=True),
        lax.all_gather(fourth, "wide", axis=0, tiled=True),
        lax.all_gather(fifth, "wide", axis=0, tiled=True),
        lax.all_gather(sixth, "wide", axis=0, tiled=True),
        lax.all_gather(seventh, "wide", axis=0, tiled=True),
    )


def settle(grads):
    first, second, third, fourth, fifth, sixth, seventh = grads
    first, second, third, fourth, fifth, sixth, seventh = (
        lax.psum_scatter(first, "wide", scatter_dimension=0, tiled=True),
        lax.psum_scatter(second, "wide", scatter_dimension=0, tiled=True),
        lax.psum_scatter(third, "wide", scatter_dimension=0, tiled=True),
        lax.psum_scatter(fourth, "wide", scatter_dimension=0, tiled=True),
        lax.psum_scatter(fifth, "wide", scatter_dimension=0, tiled=True),
        lax.psum_scatter(sixth, "wide", scatter_dimension=0, tiled=True),
        lax.psum_scatter(seventh, "wide", scatter_dimension=0, tiled=True),
    )
    return (
        lax.psum_scatter(first, "narrow", scatter_dimension=1, tiled=True),
        lax.psum_scatter(second, "narrow", scatter_dimension=1, tiled=True),
        lax.psum_scatter(third, "narrow", scatter_dimension=1, tiled=True),
        lax.psum_scatter(fourth, "narrow", scatter_dimension=1, tiled=True),
        lax.psum_scatter(fifth, "narrow", scatter_dimension=1, tiled=True),
        lax.psum_scatter(sixth, "narrow", scatter_dimension=1, tiled=True),
        lax.psum_scatter(seventh, "narrow", scatter_dimension=1, tiled=True),
    )


def local(
    inputs,
    encoded,
    target_lengths,
    memory_lengths,
    buckets,
    cotangent,
    self_inward,
    self_outward,
    cross_query,
    cross_reader,
    cross_writer,
    expand_weight,
    shrink_weight,
    norm_gains,
    bias_table,
):
    shards = (
        self_inward,
        self_outward,
        cross_query,
        cross_reader,
        cross_writer,
        expand_weight,
        shrink_weight,
    )
    inward, outward, asking, reader, writer, expand, shrink = fetch(shards)
    seqs, length, width = inputs.shape
    memory_size = encoded.shape[1]
    places = jnp.arange(length)
    causal = places[None, :] <= places[:, None]
    row_keep = (places[None, :] < target_lengths[:, None]).astype(jnp.float32)[:, :, None]
    open_keys = (jnp.arange(memory_size)[None, :] < memory_lengths[:, None])[:, None, :]
    buckets_hot = (buckets[:, :, None] == jnp.arange(bias_table.shape[0])[None, None, :]).astype(
        jnp.float32
    )
    self_extra = jnp.einsum("qkn,nh->hqk", buckets_hot, bias_table, precision=lax.Precision.HIGHEST)
    cross_extra = jnp.zeros((HEADS, 1, 1), jnp.float32)
    state = inputs.astype(jnp.float32)
    normed, pull_first = jax.vjp(norm_row, state, norm_gains[0])
    normed_first = normed.astype(jnp.bfloat16)
    self_query, self_keys, self_values = split_heads(
        project(normed_first, inward).astype(jnp.bfloat16), 3
    )
    self_mixed, self_logsum = attend_forward(self_query, self_keys, self_values, self_extra, causal)
    after_self = state + project(self_mixed, outward)
    normed, pull_second = jax.vjp(norm_row, after_self, norm_gains[1])
    normed_second = normed.astype(jnp.bfloat16)
    cross_asks = split_heads(project(normed_second, asking).astype(jnp.bfloat16), 1)[0]
    cross_keys, cross_values = split_heads(project(encoded, reader).astype(jnp.bfloat16), 2)
    cross_mixed, cross_logsum = attend_forward(
        cross_asks, cross_keys, cross_values, cross_extra, open_keys
    )
    after_cross = after_self + project(cross_mixed, writer)
    normed, pull_third = jax.vjp(norm_row, after_cross, norm_gains[2])
    normed_third = normed.astype(jnp.bfloat16)
    before = project(normed_third, expand)
    activated, pull_gelu = jax.vjp(exact_gelu, before)
    hidden = activated.astype(jnp.bfloat16)
    output = after_cross + project(hidden, shrink)
    layer_out = (output * row_keep).astype(jnp.bfloat16)
    inward, outward, asking, reader, writer, expand, shrink = fetch(shards)
    grad_output = cotangent.astype(jnp.float32) * row_keep
    grad_branch = grad_output.astype(jnp.bfloat16)
    grad_shrink = weight_grad(hidden, grad_branch)
    grad_before = pull_gelu(project_back(grad_branch, shrink))[0].astype(jnp.bfloat16)
    grad_expand = weight_grad(normed_third, grad_before)
    part, gain_third = pull_third(project_back(grad_before, expand))
    grad_cross = grad_output + part
    grad_branch = grad_cross.astype(jnp.bfloat16)
    grad_writer = weight_grad(cross_mixed, grad_branch)
    grad_mixed = split_heads(project_back(grad_branch, writer).astype(jnp.bfloat16), 1)[0]
    grad_asks, grad_keys, grad_values, unused = attend_backward(
        cross_asks,
        cross_keys,
        cross_values,
        cross_extra,
        open_keys,
        cross_logsum,
        grad_mixed,
        False,
    )
    grad_pairs = jnp.concatenate(
        (merge_heads(grad_keys), merge_heads(grad_values)), axis=-1
    ).astype(jnp.bfloat16)
    grad_reader = weight_grad(encoded, grad_pairs)
    encoded_grad = project_back(grad_pairs, reader)
    grad_asks = merge_heads(grad_asks).astype(jnp.bfloat16)
    grad_asking = weight_grad(normed_second, grad_asks)
    part, gain_second = pull_second(project_back(grad_asks, asking))
    grad_self = grad_cross + part
    grad_branch = grad_self.astype(jnp.bfloat16)
    grad_outward = weight_grad(self_mixed, grad_branch)
    grad_mixed = split_heads(project_back(grad_branch, outward).astype(jnp.bfloat16), 1)[0]
    grad_query, grad_keys, grad_values, grad_bias = attend_backward(
        self_query, self_keys, self_values, self_extra, causal, self_logsum, grad_mixed, True
    )
    table_local = jnp.einsum("hqk,qkn->nh", grad_bias, buckets_hot, precision=lax.Precision.HIGHEST)
    grad_packed = jnp.concatenate(
        (merge_heads(grad_query), merge_heads(grad_keys), merge_heads(grad_values)), axis=-1
    ).astype(jnp.bfloat16)
    grad_inward = weight_grad(normed_first, grad_packed)
    part, gain_first = pull_first(project_back(grad_packed, inward))
    inputs_grad = grad_self + part
    gains_grad, table_grad = lax.psum(
        (jnp.stack((gain_first, gain_second, gain_third)), table_local), ("wide", "narrow")
    )
    sums = settle(
        (grad_inward, grad_outward, grad_asking, grad_reader, grad_writer, grad_expand, grad_shrink)
    )
    row_parts = [jnp.sum(grad * grad, axis=1) for grad in sums]
    rows = lax.psum(
        (
            row_parts[0],
            row_parts[1],
            row_parts[2],
            row_parts[3],
            row_parts[4],
            row_parts[5],
            row_parts[6],
        ),
        "narrow",
    )
    col_parts = [jnp.sum(grad * grad, axis=0) for grad in sums]
    totals = [jnp.sum(summed) for summed in rows]
    gathered = lax.psum(
        (
            col_parts[0],
            col_parts[1],
            col_parts[2],
            col_parts[3],
            col_parts[4],
            col_parts[5],
            col_parts[6],
            totals[0],
            totals[1],
            totals[2],
            totals[3],
            totals[4],
            totals[5],
            totals[6],
        ),
        "wide",
    )
    wide_count = lax.axis_size("wide")
    narrow_count = lax.axis_size("narrow")
    results = []
    for index in range(7):
        grad = sums[index]
        full_rows = grad.shape[0] * wide_count
        full_cols = grad.shape[1] * narrow_count
        row_stat = rows[index] / full_cols + TINY
        col_stat = gathered[index] / full_rows + TINY
        mean_rows = gathered[7 + index] / (full_rows * full_cols) + TINY
        step = grad * lax.rsqrt(row_stat[:, None] * col_stat[None, :] / mean_rows)
        results.extend([grad, step, row_stat, col_stat])
    return (layer_out, inputs_grad, encoded_grad) + tuple(results) + (gains_grad, table_grad)


def solution(mesh):
    return jax.shard_map(
        local,
        mesh=mesh,
        in_specs=(
            P(("wide", "narrow"), None, None),
            P(("wide", "narrow"), None, None),
            P(("wide", "narrow")),
            P(("wide", "narrow")),
            P(),
            P(("wide", "narrow"), None, None),
            P("wide", "narrow"),
            P("wide", "narrow"),
            P("wide", "narrow"),
            P("wide", "narrow"),
            P("wide", "narrow"),
            P("wide", "narrow"),
            P("wide", "narrow"),
            P(),
            P(),
        ),
        out_specs=(
            P(("wide", "narrow"), None, None),
            P(("wide", "narrow"), None, None),
            P(("wide", "narrow"), None, None),
            P("wide", "narrow"),
            P("wide", "narrow"),
            P("wide"),
            P("narrow"),
            P("wide", "narrow"),
            P("wide", "narrow"),
            P("wide"),
            P("narrow"),
            P("wide", "narrow"),
            P("wide", "narrow"),
            P("wide"),
            P("narrow"),
            P("wide", "narrow"),
            P("wide", "narrow"),
            P("wide"),
            P("narrow"),
            P("wide", "narrow"),
            P("wide", "narrow"),
            P("wide"),
            P("narrow"),
            P("wide", "narrow"),
            P("wide", "narrow"),
            P("wide"),
            P("narrow"),
            P("wide", "narrow"),
            P("wide", "narrow"),
            P("wide"),
            P("narrow"),
            P(),
            P(),
        ),
        check_vma=False,
    )
```

profile of v0, /device:TPU:0, one launch (start us, length us, event | category | flops | bytes accessed | tf_op | source)
XLA Modules:
  0.0 1279.5 jit_solution(1545950293007169353)
XLA Ops:
  7.3 8.0 all_gather.62
  15.4 5.7 all_gather.56
  21.2 5.8 all_gather.58
  27.0 5.0 all_gather.60
  32.1 5.7 all_gather.64
  37.9 6.4 all_gather.66
  44.4 7.9 all_gather.68
  56.9 11.5 copy.134
  72.1 5.0 copy.137
  77.2 8.6 convolution_convert_fusion.2
  85.7 8.9 copy.142
  94.6 3.7 slice_bitcast_fusion
  102.4 3.9 all-gather.8.cloned.1.call-done
  106.4 5.7 convolution_convert_fusion.3
  112.1 4.3 copy.132
  122.0 48.1 %while.58 = (s32[]{:T(128)}, bf16[12,2,256,64]{2,3,0,1:T(8,128)(2,1)}, f32[12,2,256]{2,1,0:T(2,128)S(1)}, bf16[12,2,256,64]{2,3,1,0:T(8,128)(2,1)}, bf16[12,2,25...) while((s32[]{:T(128)}, ...), condition=%wide.region_4.5_spmd.clone, body=%wide.region_1.4_spmd.clone.sunk | while | flops 34831872 | bytes 2771037 | solution.py:67
  170.0 3.9 multiply_reduce_fusion.7
  173.9 11.7 all-gather.12.cloned.1.call-done
  194.6 54.0 %while.59 = (s32[]{:T(128)}, bf16[12,2,256,64]{2,3,0,1:T(8,128)(2,1)}, f32[12,2,256]{2,1,0:T(2,128)S(1)}, bf16[12,2,256,64]{2,3,1,0:T(8,128)(2,1)}, bf16[12,2,10...) while((s32[]{:T(128)}, ...), condition=%wide.region_9.10_spmd.clone, body=%wide.region_6.9_spmd.clone.sunk | while | flops 140543488 | bytes 6973537 | solution.py:67
  248.6 4.0 multiply_reduce_fusion.6
  252.6 27.0 %all-gather.18.cloned.1.call-done = bf16[768,3072]{1,0:T(8,128)(2,1)} async-done(((bf16[48,3072]{1,0:T(8,128)(2,1)}), bf16[768,3072]{1,0:T(8,128)(2,1)}) %all-gather.18.cloned.1.call-update) | async-done | bytes 4718608 | tf_op jit(solution)/shard_map/all_gather | solution.py:121
  279.6 7.2 fusion.132
  289.4 15.7 %multiply_convert_fusion.2 = (bf16[2,256,3072]{2,1,0:T(8,128)(2,1)}, f32[2,256,3072]{2,1,0:T(8,128)}) fusion(f32[2,256,3072]{2,1,0:T(8,128)S(1)} %get-tuple-element.664, u8[256,3072]{1,0:T(8,128)(4,1)S(1)} %get-tuple-element.512, u8[256,3072]{1,0:T(8,128)(4,1)S(1)} %get-tuple-element.511), kind=kLoop, calls=%fused_computation.134 | loop fusion | flops 110100480 | bytes 17301504 | tf_op jit(solution)/shard_map/convert_element_type | solution.py:206
  305.1 28.6 %all-gather.20.cloned.1.call-done = bf16[3072,768]{1,0:T(8,128)(2,1)} async-done(((bf16[192,768]{1,0:T(8,128)(2,1)}), bf16[3072,768]{1,0:T(8,128)(2,1)}) %all-gather.20.cloned.1.call-update) | async-done | bytes 4718608 | tf_op jit(solution)/shard_map/all_gather | solution.py:122
  333.7 10.3 add_convert_fusion
  344.1 6.3 multiply_reduce_fusion.2
  357.2 112.4 %while.60 = (s32[]{:T(128)}, bf16[12,2,256,64]{2,3,0,1:T(8,128)(2,1)}, bf16[12,2,1024,64]{2,3,0,1:T(8,128)(2,1)}, bf16[12,2,1024,64]{2,3,0,1:T(8,128)(2,1)}, bf1...) while((s32[]{:T(128)}, ...), condition=%wide.region_14.15_spmd.clone, body=%wide.region_12.14_spmd.clone.sunk | while | flops 340428288 | bytes 17976440 | solution.py:101
  469.5 3.9 convolution_bitcast_fusion.7
  473.6 3.9 convolution_bitcast_fusion.6
  490.6 4.7 copy.169
  495.3 4.7 copy.170
  500.0 10.2 fusion.113
  510.2 6.1 copy.193
  519.3 209.9 %while.61 = (s32[]{:T(128)}, bf16[12,2,256,64]{2,3,0,1:T(8,128)(2,1)}, bf16[12,2,256,64]{2,3,0,1:T(8,128)(2,1)}, bf16[12,2,256,64]{2,3,0,1:T(8,128)(2,1)}, f32[1...) while((s32[]{:T(128)}, ...), condition=%wide.region_19.20_spmd.clone, body=%wide.region_16.19_spmd.clone.sunk | while | flops 85523968 | bytes 9125029 | solution.py:101
  524.8 6.9 dynamic_update_slice.80
  542.3 7.0 dynamic_update_slice.80
  559.8 6.9 dynamic_update_slice.80
  577.2 6.9 dynamic_update_slice.80
  594.7 6.9 dynamic_update_slice.80
  612.1 7.0 dynamic_update_slice.80
  629.6 7.0 dynamic_update_slice.80
  647.2 6.9 dynamic_update_slice.80
  664.6 6.9 dynamic_update_slice.80
  682.0 7.0 dynamic_update_slice.80
  699.6 7.0 dynamic_update_slice.80
  717.1 6.9 dynamic_update_slice.80
  736.1 6.9 convolution_bitcast_fusion.2
  743.0 8.8 convolution_bitcast_fusion.4
  751.9 8.9 convolution_bitcast_fusion.3
  764.9 6.8 fusion.124
  771.7 67.3 %reduce-scatter.17.cloned.1.call-done = f32[48,2304]{1,0:T(8,128)} async-done(((f32[768,2304]{1,0:T(8,128)}), f32[48,2304]{1,0:T(8,128)}) %reduce-scatter.17.cloned.1.call-update) | async-done | bytes 442384 | tf_op jit(solution)/shard_map/reduce_scatter | solution.py:129
  839.1 6.5 convolution_bitcast_fusion.9
  845.6 7.1 multiply_convert_fusion.3
  852.7 101.9 %reduce-scatter.35.cloned.1.call-done = f32[48,3072]{1,0:T(8,128)} async-done(((f32[768,3072]{1,0:T(8,128)}), f32[48,3072]{1,0:T(8,128)}) %reduce-scatter.35.cloned.1.call-update) | async-done | bytes 589840 | tf_op jit(solution)/shard_map/reduce_scatter | solution.py:134
  954.6 9.6 fusion.112
  964.2 105.4 %reduce-scatter.39.cloned.1.call-done = f32[192,768]{1,0:T(8,128)} async-done(((f32[3072,768]{1,0:T(8,128)}), f32[192,768]{1,0:T(8,128)}) %reduce-scatter.39.cloned.1.call-update) | async-done | bytes 589840 | tf_op jit(solution)/shard_map/reduce_scatter | solution.py:135
  1069.7 40.8 %all-reduce = (f32[3,768]{1,0:T(4,128)}, f32[32,12]{0,1:T(8,128)}) all-reduce(f32[3,768]{1,0:T(4,128)S(1)} %pad_maximum_fusion.8, f32[32,12]{0,1:T(8,128)S(1)} %convolution_bitcast_fusion.9), channel_id=1, replica_groups=mesh['wide'=16,'narrow'=2] {'wide','narrow'}, use_global_device_ids=true, to_apply=%region_80.81 | all-reduce | flops 2688 | bytes 21504 | tf_op jit(solution)/shard_map/psum | solution.py:252
  1110.5 3.7 fusion.127
  1117.3 11.6 reduce-scatter.29.cloned.1.call-done
  1131.9 13.5 %reduce-scatter.19.cloned.1.call-done = f32[48,1152]{1,0:T(8,128)} async-done(((f32[48,2304]{1,0:T(8,128)}), f32[48,1152]{1,0:T(8,128)}) %reduce-scatter.19.cloned.1.call-update) | async-done | bytes 221200 | tf_op jit(solution)/shard_map/reduce_scatter | solution.py:138
  1146.5 17.0 %reduce-scatter.37.cloned.1.call-done = f32[48,1536]{1,0:T(8,128)} async-done(((f32[48,3072]{1,0:T(8,128)}), f32[48,1536]{1,0:T(8,128)}) %reduce-scatter.37.cloned.1.call-update) | async-done | bytes 294928 | tf_op jit(solution)/shard_map/reduce_scatter | solution.py:143
  1164.6 17.0 %reduce-scatter.41.cloned.1.call-done = f32[192,384]{1,0:T(8,128)} async-done(((f32[192,768]{1,0:T(8,128)}), f32[192,384]{1,0:T(8,128)}) %reduce-scatter.41.cloned.1.call-update) | async-done | bytes 294928 | tf_op jit(solution)/shard_map/reduce_scatter | solution.py:144
  1182.7 4.9 all-reduce.2
  1192.2 60.6 %all-reduce.1 = (f32[]{:T(128)}, f32[1152]{0:T(1024)}, f32[]{:T(128)}, f32[384]{0:T(512)}, f32[]{:T(128)}, /*index=5*/f32[384]{0:T(512)}, f32[]{:T(128)}, f32[76...) all-reduce(f32[]{:T(128)} %get-tuple-element.672, ...), channel_id=1, replica_groups=mesh['wide'=16,'narrow'=2] {'wide'}, use_global_device_ids=true, to_apply=%region_28.29 | all-reduce | flops 4999 | bytes 39992 | tf_op jit(solution)/shard_map/psum | solution.py:273
  (549 shorter events, 432.0 us)
Async XLA Ops:
  7.2 70.0 %copy-start = (bf16[2,1024,768]{2,1,0:T(8,128)(2,1)S(1)}, bf16[2,1024,768]{2,1,0:T(8,128)(2,1)}, u32[]{:S(2)}) copy-start(bf16[2,1024,768]{2,1,0:T(8,128)(2,1)} %param.24) | copy-start | bytes 9437188
  7.2 69.9 %all-gather.14.cloned.1.call-start = ((), (), s32[]{:S(2)}) async-start(), calls=%async_computation.17 | async-start | bytes 2506752 | tf_op jit(solution)/shard_map/all_gather | solution.py:119
  15.3 91.1 %all-gather.8.cloned.1.call-start = ((), (), s32[]{:S(2)}) async-start(), calls=%async_computation.14 | async-start | bytes 3760128 | tf_op jit(solution)/shard_map/all_gather | solution.py:116
  21.1 148.9 %all-gather.10.cloned.1.call-start = ((), (), s32[]{:S(2)}) async-start(), calls=%async_computation.15 | async-start | bytes 1253376 | tf_op jit(solution)/shard_map/all_gather | solution.py:117
  27.0 158.6 %all-gather.12.cloned.1.call-start = ((), (), s32[]{:S(2)}) async-start(), calls=%async_computation.16 | async-start | bytes 1253376 | tf_op jit(solution)/shard_map/all_gather | solution.py:118
  32.0 216.6 %all-gather.16.cloned.1.call-start = ((), (), s32[]{:S(2)}) async-start(), calls=%async_computation.18 | async-start | bytes 1253376 | tf_op jit(solution)/shard_map/all_gather | solution.py:120
  37.8 241.8 %all-gather.18.cloned.1.call-start = ((), (), s32[]{:S(2)}) async-start(), calls=%async_computation.19 | async-start | bytes 5013504 | tf_op jit(solution)/shard_map/all_gather | solution.py:121
  44.3 289.4 %all-gather.20.cloned.1.call-start = ((), (), s32[]{:S(2)}) async-start(), calls=%async_computation.20 | async-start | bytes 5013504 | tf_op jit(solution)/shard_map/all_gather | solution.py:122
  52.3 708.5 %reduce-scatter.25.cloned.1.call-start = ((), (), s32[]{:S(2)}) async-start(), calls=%async_computation.25 | async-start | bytes 2506752 | tf_op jit(solution)/shard_map/reduce_scatter | solution.py:131
  54.6 13.8 %copy-start.18 = (f32[2,256]{1,0:T(2,128)}, f32[2,256]{1,0:T(2,128)S(1)}, u32[]{:S(2)}) copy-start(f32[2,256]{1,0:T(2,128)S(1)} %fusion.128) | copy-start | bytes 6148
  55.7 12.7 copy-start.11
  55.7 12.7 copy-start.21
  72.1 5.0 copy-start.25
  185.6 9.0 copy-start.15
  286.8 2.7 copy-start.8
  333.7 10.3 copy-start.2
  344.0 6.4 copy-start.10
  344.1 6.4 copy-start.14
  350.4 1.7 copy-start.13
  351.0 1.1 copy-start.6
  473.5 287.9 %reduce-scatter.31.cloned.1.call-start = ((), (), s32[]{:S(2)}) async-start(), calls=%async_computation.28 | async-start | bytes 2506752 | tf_op jit(solution)/shard_map/reduce_scatter | solution.py:133
  477.5 284.5 %reduce-scatter.21.cloned.1.call-start = ((), (), s32[]{:S(2)}) async-start(), calls=%async_computation.23 | async-start | bytes 2506752 | tf_op jit(solution)/shard_map/reduce_scatter | solution.py:130
  477.5 3.4 copy-start.4
  477.5 3.4 copy-start.7
  480.9 1.6 copy-start.9
  481.3 1.1 copy-start.5
  484.7 277.9 %reduce-scatter.43.cloned.1.call-start = ((), (), s32[]{:S(2)}) async-start(), calls=%async_computation.34 | async-start | bytes 5013504
  516.3 322.7 %reduce-scatter.17.cloned.1.call-start = ((), (), s32[]{:S(2)}) async-start(), calls=%async_computation.21 | async-start | bytes 7520256 | tf_op jit(solution)/shard_map/reduce_scatter | solution.py:129
  522.9 0.8 copy-start.1
  540.4 0.8 copy-start.1
  557.9 0.8 copy-start.1
  575.3 0.8 copy-start.1
  592.8 0.8 copy-start.1
  610.2 0.8 copy-start.1
  627.7 0.8 copy-start.1
  645.3 0.8 copy-start.1
  662.7 0.8 copy-start.1
  680.1 0.8 copy-start.1
  697.7 0.8 copy-start.1
  715.2 0.8 copy-start.1
  743.0 211.6 %reduce-scatter.35.cloned.1.call-start = ((), (), s32[]{:S(2)}) async-start(), calls=%async_computation.30 | async-start | bytes 10027008 | tf_op jit(solution)/shard_map/reduce_scatter | solution.py:134
  751.9 317.8 %reduce-scatter.39.cloned.1.call-start = ((), (), s32[]{:S(2)}) async-start(), calls=%async_computation.32 | async-start | bytes 10027008 | tf_op jit(solution)/shard_map/reduce_scatter | solution.py:135
  760.8 353.4 %reduce-scatter.27.cloned.1.call-start = ((), (), s32[]{:S(2)}) async-start(), calls=%async_computation.26 | async-start | bytes 221184 | tf_op jit(solution)/shard_map/reduce_scatter | solution.py:140
  761.4 353.8 %reduce-scatter.33.cloned.1.call-start = ((), (), s32[]{:S(2)}) async-start(), calls=%async_computation.29 | async-start | bytes 221184 | tf_op jit(solution)/shard_map/reduce_scatter | solution.py:142
  762.0 354.3 %reduce-scatter.23.cloned.1.call-start = ((), (), s32[]{:S(2)}) async-start(), calls=%async_computation.24 | async-start | bytes 221184 | tf_op jit(solution)/shard_map/reduce_scatter | solution.py:139
  762.5 366.3 %reduce-scatter.29.cloned.1.call-start = ((), (), s32[]{:S(2)}) async-start(), calls=%async_computation.27 | async-start | bytes 1179648 | tf_op jit(solution)/shard_map/reduce_scatter | solution.py:141
  764.8 74.3 %copy-start.12 = (s32[256,256]{0,1:T(8,128)S(1)}, s32[256,256]{0,1:T(8,128)}, u32[]{:S(2)}) copy-start(s32[256,256]{0,1:T(8,128)} %copy-done.11) | copy-start | bytes 786436
  764.8 380.6 %reduce-scatter.19.cloned.1.call-start = ((), (), s32[]{:S(2)}) async-start(), calls=%async_computation.22 | async-start | bytes 663552 | tf_op jit(solution)/shard_map/reduce_scatter | solution.py:138
  839.0 324.4 %reduce-scatter.37.cloned.1.call-start = ((), (), s32[]{:S(2)}) async-start(), calls=%async_computation.31 | async-start | bytes 884736 | tf_op jit(solution)/shard_map/reduce_scatter | solution.py:143
  839.1 6.5 copy-start.3
  845.6 109.0 %copy-start.19 = (f32[2,256]{1,0:T(2,128)S(1)}, f32[2,256]{1,0:T(2,128)}, u32[]{:S(2)}) copy-start(f32[2,256]{1,0:T(2,128)} %copy-done.18) | copy-start | bytes 6148
  954.6 227.0 %reduce-scatter.41.cloned.1.call-start = ((), (), s32[]{:S(2)}) async-start(), calls=%async_computation.33 | async-start | bytes 884736 | tf_op jit(solution)/shard_map/reduce_scatter | solution.py:144
  1252.7 19.4 %copy-start.22 = (f32[384]{0:T(512)}, f32[384]{0:T(512)S(1)}, u32[]{:S(2)}) copy-start(f32[384]{0:T(512)S(1)} %multiply_add_fusion.3) | copy-start | bytes 4612
  1252.7 19.4 %copy-start.16 = (f32[1536]{0:T(1024)}, f32[1536]{0:T(1024)S(1)}, u32[]{:S(2)}) copy-start(f32[1536]{0:T(1024)S(1)} %multiply_add_fusion) | copy-start | bytes 18436
  1255.3 16.9 %copy-start.20 = (f32[768]{0:T(1024)}, f32[768]{0:T(1024)S(1)}, u32[]{:S(2)}) copy-start(f32[768]{0:T(1024)S(1)} %multiply_add_fusion.2) | copy-start | bytes 9220
  1258.6 13.5 %copy-start.23 = (f32[384]{0:T(512)}, f32[384]{0:T(512)S(1)}, u32[]{:S(2)}) copy-start(f32[384]{0:T(512)S(1)} %multiply_add_fusion.5) | copy-start | bytes 4612
  1260.0 12.2 copy-start.24
  1261.3 10.8 copy-start.17
Sparse Core Ops, SparseCore 0:
  15.4 42.6 all-gather.13
  60.4 45.9 all-gather.7
  108.7 37.3 all-gather.9
  148.2 37.3 all-gather.11
  187.7 37.5 all-gather.15
  227.4 52.1 all-gather.17
  281.9 51.7 all-gather.19
  473.6 61.4 reduce-scatter.24
  539.4 62.0 reduce-scatter.30
  605.1 61.9 reduce-scatter.20
  671.5 74.5 reduce-scatter.42
  749.9 89.0 reduce-scatter.16
  843.6 110.8 reduce-scatter.34
  958.5 111.0 reduce-scatter.38
  1072.4 10.2 reduce-scatter.26
  1085.3 10.4 reduce-scatter.32
  1098.5 10.5 reduce-scatter.22
  1111.4 17.4 reduce-scatter.28
  1131.7 13.6 reduce-scatter.18
  1148.2 15.2 reduce-scatter.36
  1166.3 15.2 reduce-scatter.40
where the time goes:
time: 1300 us; the launch traced here: 1280 us
  matrix products  416 us (32%)
  waiting for transfers between devices  407 us (31%)
  local copies, waits for them, and re-layouts  220 us (17%)
  blocking collectives  151 us (12%)
  other arithmetic  63.8 us (5%)
  between operations  20 us (2%)
    reduce_scatter x1, waiting for transfers between devices, settle(): lax.psum_scatter(seventh, 'wide', scatter_dimension=0, tiled=True)  105 us
    reduce_scatter x1, waiting for transfers between devices, settle(): lax.psum_scatter(sixth, 'wide', scatter_dimension=0, tiled=True)  102 us
    dynamic_update_slice x24, local copies, waits for them, and re-layouts, attend_backward(): return lax.map(one_head, (query, keys, values, extra, logsum, grad_mixed))  95.1 us
    dot_general x48, matrix products, head_scores(): jnp.einsum('sqd,skd->sqk', query, keys, preferred_element_type=jnp.float32)  69.5 us
    reduce_scatter x1, waiting for transfers between devices, settle(): lax.psum_scatter(first, 'wide', scatter_dimension=0, tiled=True)  67.3 us
    psum x1, blocking collectives, local(): lax.psum((col_parts[0], col_parts[1], col_parts[2], col_parts[3], col_par...  60.6 us
    dot_general x24, matrix products, one_head(): jnp.einsum('sqk,skd->sqd', probs, head_values, preferred_element_type=jnp...  47.8 us
    dot_general x7, matrix products, weight_grad(): jnp.einsum('std,ste->de', left, grad, preferred_element_type=jnp.float32)  44.8 us
  transfers between devices with their start and end apart: 21, of which 11 were waited for; matrix products, arithmetic and copies ran while one was open for 41% of the time, Pallas kernels for 0%

commit v1 on v0

v1 whole, which is shorter than its diff:
```python
import functools

import jax
import jax.numpy as jnp
from jax import lax
from jax.experimental import pallas as pl
from jax.experimental.pallas import tpu as pltpu
from jax.sharding import PartitionSpec as P

HEADS = 12
DH = 64
EPS = 1e-06
TINY = 1e-30
NEGATIVE = -1e30
SCALE = DH ** (-0.5)

BF = jnp.bfloat16
F32 = jnp.float32
BOTH = ("wide", "narrow")
VMEM_LIMIT = 56 * 1024 * 1024
KEY_TILE = 256

COUNTS = {
    "inward": 3,
    "outward": 1,
    "query": 1,
    "reader": 2,
    "writer": 1,
    "expand": 4,
    "shrink": 4,
}
NAMES = ("inward", "outward", "query", "reader", "writer", "expand", "shrink")
GATHERS = (
    ("x", ("inward", "outward", "query")),
    ("y", ("reader", "writer")),
    ("x", ("expand",)),
    ("y", ("shrink",)),
)


def nn(left, right):
    return lax.dot_general(left, right, (((1,), (0,)), ((), ())), preferred_element_type=F32)


def nt(left, right):
    return lax.dot_general(left, right, (((1,), (1,)), ((), ())), preferred_element_type=F32)


def tn(left, right):
    return lax.dot_general(left, right, (((0,), (0,)), ((), ())), preferred_element_type=F32)


VM = pl.BlockSpec(memory_space=pltpu.VMEM)
SM = pl.BlockSpec(memory_space=pltpu.SMEM)
HB = pl.BlockSpec(memory_space=pl.ANY)


def launch(body, ins, outs, scratch=(), grid=None, alias=None, gflop=1.0, name=None):
    arrays = [a for a, _ in ins]
    return pl.pallas_call(
        body,
        grid=grid if grid is not None else (),
        in_specs=[s for _, s in ins],
        out_specs=[s for _, s in outs],
        out_shape=[o for o, _ in outs],
        scratch_shapes=list(scratch),
        input_output_aliases=alias or {},
        compiler_params=pltpu.CompilerParams(vmem_limit_bytes=VMEM_LIMIT),
        cost_estimate=pl.CostEstimate(
            flops=int(gflop * 1e9), bytes_accessed=1 << 22, transcendentals=0
        ),
        name=name,
    )(*arrays)


def shape(dims, dtype):
    return jax.ShapeDtypeStruct(tuple(dims), dtype)


def weight_scratch(name, width):
    if name == "shrink":
        return pltpu.VMEM((4, 2, 2, 4, width // 16, width), BF)
    return pltpu.VMEM((4, 2, 2, width // 16, width * COUNTS[name]), BF)


class Held:
    def __init__(self, arrays, first, start):
        self.arrays, self.first, self.start = tuple(arrays), first, start

    def ins(self):
        return [(a, HB) for a in self.arrays]


def load(name, held, refs, scratch, me, sem):
    if len(refs) == 1:
        pltpu.make_async_copy(refs[0], scratch, sem).start()
        return
    count = COUNTS[name]
    piece = refs[0].shape[-1]
    for a in range(2):
        for b in range(2):
            for k in range(2):
                c = me[2] ^ b
                if held.first == "x":
                    x, y = me[1] ^ k, me[3] ^ a
                else:
                    x, y = me[1] ^ a, me[3] ^ k
                for p in range(count):
                    src = refs[a * 2 + b].at[k, :, held.start + p]
                    if name == "shrink":
                        cols = pl.ds(pl.multiple_of(y * piece, 128), piece)
                        dst = scratch.at[:, x, c, p, :, cols]
                    else:
                        cols = pl.ds(pl.multiple_of((y * count + p) * piece, 128), piece)
                        dst = scratch.at[:, x, c, :, cols]
                    pltpu.make_async_copy(src, dst, sem).start()


def arrived(scratch, sem):
    pltpu.make_async_copy(scratch, scratch, sem).wait()


def store(name, scratch, outs, start, me, sem):
    if len(outs) == 1:
        pltpu.make_async_copy(scratch, outs[0], sem).start()
        return
    count = COUNTS[name]
    piece = outs[0].shape[-1]
    for b in range(2):
        c = me[2] ^ b
        for y in range(2):
            for p in range(count):
                if name == "shrink":
                    src = scratch.at[:, :, c, p, :, pl.ds(y * piece, piece)]
                else:
                    src = scratch.at[:, :, c, :, pl.ds((y * count + p) * piece, piece)]
                pltpu.make_async_copy(src, outs[b].at[:, :, y, start + p], sem).start()


def flat(block):
    return block.reshape(-1, block.shape[-1])


def put_rows(scratch, value, cols):
    scratch[:, :, :, :, cols] = value.reshape(scratch.shape[:4] + (value.shape[-1],))


def normed(values, gain):
    r = lax.rsqrt(jnp.mean(values * values, axis=-1, keepdims=True) + EPS)
    return values * r * gain


def norm_back(values, gain, grad):
    r = lax.rsqrt(jnp.mean(values * values, axis=-1, keepdims=True) + EPS)
    inner = jnp.mean(values * gain * grad, axis=-1, keepdims=True)
    back = r * gain * grad - values * (r * r * r * inner)
    return back, jnp.sum(grad * values * r, axis=0, keepdims=True)


def prepare_kernel(lens, x, cot, gains, buckets, table, n1, kept, bias):
    rows = cot.shape[1]
    for s in range(x.shape[0]):
        values = x[s].astype(F32)
        n1[s * rows : (s + 1) * rows, :] = normed(values, gains[0:1, :]).astype(BF)
        keep = lax.broadcasted_iota(jnp.int32, (rows, 1), 0) < lens[s]
        kept[s * rows : (s + 1) * rows, :] = jnp.where(keep, cot[s].astype(F32), 0.0).astype(BF)
    half = 128
    heads = bias.shape[0]

    @pl.loop(0, rows // 8)
    def _(step):
        start = pl.multiple_of(step * 8, 8)
        for side in range(rows // half):
            which = buckets[pl.ds(start, 8), side * half : (side + 1) * half]
            key = start + lax.broadcasted_iota(jnp.int32, (8, half), 0)
            query = side * half + lax.broadcasted_iota(jnp.int32, (8, half), 1)
            for h in range(heads):
                row = jnp.broadcast_to(table[h : h + 1, :], (8, half))
                found = jnp.take_along_axis(row, which, axis=1)
                bias[h, pl.ds(start, 8), side * half : (side + 1) * half] = jnp.where(
                    key <= query, found, NEGATIVE
                )


def head_parts(block):
    lane = lax.broadcasted_iota(jnp.int32, block.shape, 1)
    zero = jnp.zeros_like(block)
    return jnp.where(lane < DH, block, zero), jnp.where(lane < DH, zero, block)


def forward_pair(query, keys, values, fix, mixed, logsum):
    parts = head_parts(query * jnp.asarray(SCALE, BF))
    tops = []
    for h in range(2):
        scores = fix(nt(keys, parts[h]), h)
        highest = jnp.max(scores, axis=0, keepdims=True)
        weights = jnp.exp(scores - highest)
        total = jnp.sum(weights, axis=0, keepdims=True)
        raw = tn(values, weights.astype(BF))
        tops.append(raw[h * DH : (h + 1) * DH, :] * (1.0 / total))
        logsum[0, h : h + 1, :] = highest + jnp.log(total)
    mixed[...] = jnp.concatenate(tops, axis=0).T.astype(BF)


def backward_pair(query, keys, values, grad, fix, logsum, each):
    scaled = head_parts(query * jnp.asarray(SCALE, BF))
    grads = head_parts(grad)
    grad_keys = grad_values = 0.0
    tops = []
    for h in range(2):
        scores = fix(nt(keys, scaled[h]), h)
        probs = jnp.exp(scores - logsum[0, h : h + 1, :])
        grad_probs = nt(values, grads[h])
        inner = jnp.sum(probs * grad_probs, axis=0, keepdims=True)
        grad_scores = (probs * (grad_probs - inner)).astype(BF)
        each(h, grad_scores)
        grad_values = grad_values + nn(probs.astype(BF), grads[h])
        grad_keys = grad_keys + nn(grad_scores, scaled[h])
        raw = tn(keys, grad_scores)
        tops.append(raw[h * DH : (h + 1) * DH, :] * SCALE)
    return jnp.concatenate(tops, axis=0).T, grad_keys, grad_values


def self_forward_kernel(query, keys, values, bias, mixed, logsum):
    def fix(scores, h):
        return scores + bias[h]

    forward_pair(query[...], keys[...], values[...], fix, mixed, logsum)


def self_backward_kernel(
    query, keys, values, grad, bias, logsum, grad_query, grad_keys, grad_values, grad_bias
):
    first = pl.program_id(1) == 0

    def fix(scores, h):
        return scores + bias[h]

    def each(h, grad_scores):
        grown = grad_scores.astype(F32)
        grad_bias[h] = jnp.where(first, grown, grad_bias[h] + grown)

    gq, gk, gv = backward_pair(query[...], keys[...], values[...], grad[...], fix, logsum, each)
    grad_query[...] = gq.astype(BF)
    grad_keys[...] = gk.astype(BF)
    grad_values[...] = gv.astype(BF)


def masked_last(valid, size):
    def fix(scores, h):
        head, tail = scores[: size - KEY_TILE], scores[size - KEY_TILE :]
        place = size - KEY_TILE + lax.broadcasted_iota(jnp.int32, tail.shape, 0)
        tail = jnp.where(place < valid, tail, NEGATIVE)
        return jnp.concatenate((head, tail), axis=0) if size > KEY_TILE else tail

    return fix


def cross_forward_kernel(lens, query, keys, values, mixed, logsum):
    valid = lens[pl.program_id(0)]
    for tiles in range(1, keys.shape[0] // KEY_TILE + 1):

        @pl.when((valid + KEY_TILE - 1) // KEY_TILE == tiles)
        def _():
            size = tiles * KEY_TILE
            forward_pair(
                query[...], keys[:size], values[:size], masked_last(valid, size), mixed, logsum
            )


def cross_backward_kernel(
    lens, query, keys, values, grad, logsum, grad_query, grad_keys, grad_values
):
    valid = lens[pl.program_id(0)]
    for tiles in range(1, keys.shape[0] // KEY_TILE + 1):

        @pl.when((valid + KEY_TILE - 1) // KEY_TILE == tiles)
        def _():
            size = tiles * KEY_TILE
            gq, gk, gv = backward_pair(
                query[...],
                keys[:size],
                values[:size],
                grad[...],
                masked_last(valid, size),
                logsum,
                lambda h, g: None,
            )
            grad_query[...] = gq.astype(BF)
            grad_keys[:size] = gk.astype(BF)
            grad_values[:size] = gv.astype(BF)


def pair_spec(rows, base=0, flip=False):
    if flip:
        return pl.BlockSpec((rows, 128), lambda p, s: (s, base + p))
    return pl.BlockSpec((rows, 128), lambda s, p: (s, base + p))


def inward_kernel(held, me, n1, *rest):
    refs, (packed, weight, sem) = rest[: len(held.arrays)], rest[len(held.arrays) :]
    load("inward", held, refs, weight, me, sem)
    arrived(weight, sem)
    size = n1.shape[1]
    left = n1[...]
    for block in range(3):
        cols = slice(block * size, (block + 1) * size)
        packed[:, cols] = nn(left, flat(weight[..., cols])).astype(BF)


def memory_kernel(held, me, lens, encoded, *rest):
    refs, (pairs, weight, sem) = rest[: len(held.arrays)], rest[len(held.arrays) :]
    step = pl.program_id(0)
    tiles = pl.num_programs(0) // lens.shape[0]

    @pl.when(step == 0)
    def _():
        load("reader", held, refs, weight, me, sem)
        arrived(weight, sem)

    @pl.when(lax.rem(step, tiles) * KEY_TILE < lens[step // tiles])
    def _():
        size = encoded.shape[1]
        left = encoded[...]
        for block in range(2):
            cols = slice(block * size, (block + 1) * size)
            pairs[:, cols] = nn(left, flat(weight[..., cols])).astype(BF)


def middle_kernel(held_out, held_query, me, x, mixed, gains, *rest):
    k = len(held_out.arrays)
    refs_out, refs_query = rest[:k], rest[k : 2 * k]
    after, n2, asks, weight_out, weight_query, sems = rest[2 * k :]
    load("outward", held_out, refs_out, weight_out, me, sems.at[0])
    load("query", held_query, refs_query, weight_query, me, sems.at[1])
    arrived(weight_out, sems.at[0])
    values = x[...].astype(F32) + nn(mixed[...], flat(weight_out[...]))
    after[...] = values
    second = normed(values, gains[1:2, :]).astype(BF)
    n2[...] = second
    arrived(weight_query, sems.at[1])
    asks[...] = nn(second, flat(weight_query[...])).astype(BF)


def gelu_parts(v):
    phi = 0.5 * (1.0 + lax.erf(v * (0.5**0.5)))
    density = jnp.exp(-0.5 * v * v) * 0.3989422804014327
    return v * phi, phi + v * density


def widen_kernel(held_writer, held_expand, me, after_self, mixed, gains, kept, *rest):
    k = len(held_writer.arrays)
    refs_writer, refs_expand = rest[:k], rest[k : 2 * k]
    outs = rest[2 * k :]
    after_cross, n3, hidden, slope = outs[:4]
    grads, (weight_writer, weight_expand, shrink_grad, sems) = outs[4:-4], outs[-4:]
    load("writer", held_writer, refs_writer, weight_writer, me, sems.at[0])
    load("expand", held_expand, refs_expand, weight_expand, me, sems.at[1])
    arrived(weight_writer, sems.at[0])
    values = after_self[...] + nn(mixed[...], flat(weight_writer[...]))
    after_cross[...] = values
    n3[...] = normed(values, gains[2:3, :]).astype(BF)
    arrived(weight_expand, sems.at[1])
    size = n3.shape[1]

    @pl.loop(0, 4)
    def _(z):
        cols = pl.ds(pl.multiple_of(z * size, 128), size)
        before = nn(n3[...], flat(weight_expand[:, :, :, :, cols]))
        active, gate = gelu_parts(before)
        active = active.astype(BF)
        hidden[:, cols] = active
        slope[:, cols] = gate.astype(BF)
        grad = tn(active, kept[...]).astype(BF)
        shrink_grad[z] = grad.reshape(shrink_grad.shape[1:])

    store("shrink", shrink_grad, grads, 0, me, sems.at[2])
    arrived(shrink_grad, sems.at[2])


def narrow_kernel(
    held_shrink, held_expand, me, lens, after_cross, n3, hidden, slope, kept, gains, *rest
):
    k = len(held_shrink.arrays)
    refs_shrink, refs_expand = rest[:k], rest[k : 2 * k]
    outs = rest[2 * k :]
    layer_out, grad_cross, gain_part = outs[:3]
    grads, (weight_shrink, weight_expand, expand_grad, grad_norm, total, sems) = (
        outs[3:-6],
        outs[-6:],
    )
    load("shrink", held_shrink, refs_shrink, weight_shrink, me, sems.at[0])
    load("expand", held_expand, refs_expand, weight_expand, me, sems.at[1])
    size = n3.shape[1]
    total[...] = after_cross[...]
    grad_norm[...] = jnp.zeros_like(grad_norm)
    arrived(weight_shrink, sems.at[0])
    arrived(weight_expand, sems.at[1])

    @pl.loop(0, 4)
    def _(z):
        cols = pl.ds(pl.multiple_of(z * size, 128), size)
        shrink_rows = flat(weight_shrink[z])
        grad = (slope[:, cols].astype(F32) * nt(kept[...], shrink_rows)).astype(BF)
        put_rows(expand_grad, tn(n3[...], grad).astype(BF), cols)
        grad_norm[...] += nt(grad, flat(weight_expand[:, :, :, :, cols]))
        total[...] += nn(hidden[:, cols], shrink_rows)

    store("expand", expand_grad, grads, 0, me, sems.at[2])
    rows = total.shape[0] // lens.shape[0]
    for s in range(lens.shape[0]):
        part = slice(s * rows, (s + 1) * rows)
        keep = lax.broadcasted_iota(jnp.int32, (rows, 1), 0) < lens[s]
        layer_out[s] = jnp.where(keep, total[part, :], 0.0).astype(BF)
    back, gain = norm_back(after_cross[...], gains[2:3, :], grad_norm[...])
    grad_cross[...] = kept[...].astype(F32) + back
    gain_part[...] = gain
    arrived(expand_grad, sems.at[2])


def writer_back_kernel(held, me, grad_cross, mixed, *rest):
    k = len(held.arrays)
    refs, outs = rest[:k], rest[k:]
    grad_mixed, grads, (weight, grad_scratch, sems) = outs[0], outs[1:-3], outs[-3:]
    load("writer", held, refs, weight, me, sems.at[0])
    branch = grad_cross[...].astype(BF)
    put_rows(grad_scratch, tn(mixed[...], branch).astype(BF), slice(None))
    store("writer", grad_scratch, grads, 0, me, sems.at[1])
    arrived(weight, sems.at[0])
    grad_mixed[...] = nt(branch, flat(weight[...])).astype(BF)
    arrived(grad_scratch, sems.at[1])


def query_back_kernel(
    packed_mode,
    held_query,
    held_out,
    me,
    grad_asks,
    n2,
    after_self,
    grad_cross,
    mixed,
    gains,
    *rest,
):
    k = len(held_query.arrays)
    refs_query, refs_out = rest[:k], rest[k : 2 * k]
    rest = rest[2 * k :]
    if packed_mode:
        rest = rest[2:]
    grad_self, grad_mixed, gain_part = rest[:3]
    weight_query, weight_out, query_grad, out_grad, sems = rest[-5:]
    grads = rest[3:-5]
    load("query", held_query, refs_query, weight_query, me, sems.at[0])
    load("outward", held_out, refs_out, weight_out, me, sems.at[1])
    put_rows(query_grad, tn(n2[...], grad_asks[...]).astype(BF), slice(None))
    store("query", query_grad, grads if packed_mode else grads[:1], 1, me, sems.at[2])
    arrived(weight_query, sems.at[0])
    back, gain = norm_back(
        after_self[...], gains[1:2, :], nt(grad_asks[...], flat(weight_query[...]))
    )
    total = grad_cross[...] + back
    grad_self[...] = total
    gain_part[...] = gain
    branch = total.astype(BF)
    arrived(weight_out, sems.at[1])
    grad_mixed[...] = nt(branch, flat(weight_out[...])).astype(BF)
    put_rows(out_grad, tn(mixed[...], branch).astype(BF), slice(None))
    store("outward", out_grad, grads if packed_mode else grads[1:], 2, me, sems.at[3])
    arrived(query_grad, sems.at[2])
    arrived(out_grad, sems.at[3])


def inward_grad_kernel(me, n1, gq, gk, gv, *rest):
    grads, (scratch, sem) = rest[:-2], rest[-2:]
    size = n1.shape[1]
    for block, grad in enumerate((gq, gk, gv)):
        cols = slice(block * size, (block + 1) * size)
        put_rows(scratch, tn(n1[...], grad[...]).astype(BF), cols)
    store("inward", scratch, grads, 0, me, sem)
    arrived(scratch, sem)


def inputs_grad_kernel(held, me, x, gq, gk, gv, grad_self, gains, *rest):
    k = len(held.arrays)
    refs, (out, gain_part, weight, sem) = rest[:k], rest[k:]
    load("inward", held, refs, weight, me, sem)
    arrived(weight, sem)
    size = x.shape[1]
    total = 0.0
    for block, grad in enumerate((gq, gk, gv)):
        cols = slice(block * size, (block + 1) * size)
        total = total + nt(grad[...], flat(weight[..., cols]))
    back, gain = norm_back(x[...].astype(F32), gains[0:1, :], total)
    out[...] = grad_self[...] + back
    gain_part[...] = gain


def reader_grad_kernel(packed_mode, me, lens, encoded, gk, gv, *rest):
    if packed_mode:
        rest = rest[2:]
    grads, (scratch, total, sem) = rest[:-3], rest[-3:]
    step = pl.program_id(0)
    steps = pl.num_programs(0)
    tiles = steps // lens.shape[0]
    size = encoded.shape[1]

    @pl.when(step == 0)
    def _():
        total[...] = jnp.zeros_like(total)

    @pl.when(lax.rem(step, tiles) * KEY_TILE < lens[step // tiles])
    def _():
        left = encoded[...]
        total[:, :size] += tn(left, gk[...])
        total[:, size:] += tn(left, gv[...])

    @pl.when(step == steps - 1)
    def _():
        put_rows(scratch, total[...].astype(BF), slice(None))
        store("reader", scratch, grads, 3, me, sem)
        arrived(scratch, sem)


def encoded_grad_kernel(held, me, lens, gk, gv, *rest):
    refs, (out, weight, sem) = rest[: len(held.arrays)], rest[len(held.arrays) :]
    step = pl.program_id(0)
    tiles = pl.num_programs(0) // lens.shape[0]
    valid = lax.rem(step, tiles) * KEY_TILE < lens[step // tiles]
    size = gk.shape[1]

    @pl.when(step == 0)
    def _():
        load("reader", held, refs, weight, me, sem)
        arrived(weight, sem)

    @pl.when(valid)
    def _():
        out[...] = nt(gk[...], flat(weight[..., :size])) + nt(gv[...], flat(weight[..., size:]))

    @pl.when(jnp.logical_not(valid))
    def _():
        out[...] = jnp.zeros_like(out)


def table_kernel(buckets, grad_bias, out):
    heads = grad_bias.shape[0]

    @pl.loop(0, out.shape[0])
    def _(b):
        hit = buckets[...] == b
        for h in range(heads):
            out[b, h : h + 1, :] = jnp.sum(
                jnp.where(hit, grad_bias[h], 0.0), axis=0, keepdims=True
            )


class Hyper:
    MASKS = {"y": 1, "c": 2, "x": 4, "z1": 8, "z2": 16}

    def __init__(self):
        wide = lax.axis_index("wide")
        self.z, self.x, self.c = wide // 4, (wide // 2) % 2, wide % 2
        self.y = lax.axis_index("narrow")
        self.me = jnp.stack((self.z, self.x, self.c, self.y)).astype(jnp.int32)

    def swap(self, value, bit):
        mask = self.MASKS[bit]
        return lax.ppermute(value, BOTH, [(i, i ^ mask) for i in range(32)])

    def gather(self, shard, first):
        second = "y" if first == "x" else "x"
        other = self.swap(shard, "z1")
        pair = jnp.where(
            self.z % 2 == 0, jnp.stack((shard, other)), jnp.stack((other, shard))
        )
        other = self.swap(pair, "z2")
        quad = jnp.where(
            self.z // 2 == 0, jnp.concatenate((pair, other)), jnp.concatenate((other, pair))
        )
        near = jnp.stack((quad, self.swap(quad, first)))
        far = self.swap(near, second)
        return near, self.swap(near, "c"), far, self.swap(far, "c")

    def scatter(self, keep, send, first):
        where = {"x": self.x, "y": self.y}
        axis = {"x": 1, "y": 2}
        second = "y" if first == "x" else "x"
        parts = [keep, self.swap(send, "c")]

        def add(pick):
            return sum(pick(p).astype(F32) for p in parts)

        pick = functools.partial(lax.dynamic_slice_in_dim, slice_size=1, axis=axis[first])
        sent = add(lambda p: pick(p, 1 - where[first])).astype(BF)
        other = self.swap(sent, first)
        parts = [pick(p, where[first]) for p in parts] + [other]
        pick2 = functools.partial(lax.dynamic_slice_in_dim, slice_size=1, axis=axis[second])
        sent = add(lambda p: pick2(p, 1 - where[second])).astype(BF)
        other = self.swap(sent, second)
        parts = [pick2(p, where[second]) for p in parts] + [other]
        half = self.z // 2
        pick3 = functools.partial(lax.dynamic_slice_in_dim, slice_size=2, axis=0)
        sent = add(lambda p: pick3(p, (1 - half) * 2)).astype(BF)
        other = self.swap(sent, "z2")
        parts = [pick3(p, half * 2) for p in parts] + [other]
        low = self.z % 2
        pick4 = functools.partial(lax.dynamic_slice_in_dim, slice_size=1, axis=0)
        sent = add(lambda p: pick4(p, 1 - low)).astype(BF)
        other = self.swap(sent, "z1")
        parts = [pick4(p, low) for p in parts] + [other]
        return add(lambda p: p)[0, 0, 0]

    def total(self, value, bits):
        for bit in bits:
            value = value + self.swap(value, bit)
        return value


def cut(name, shard, width):
    count = COUNTS[name]
    if name == "shrink":
        return shard.reshape(count, shard.shape[0] // count, shard.shape[1])
    rows, cols = shard.shape
    return jnp.transpose(shard.reshape(rows, count, cols // count), (1, 0, 2))


def uncut(name, pieces):
    count, rows, cols = pieces.shape
    if name == "shrink":
        return pieces.reshape(count * rows, cols)
    return jnp.transpose(pieces, (1, 0, 2)).reshape(rows, count * cols)


def whole_shape(name, width):
    if name == "shrink":
        return (4, 2, 2, 4, width // 16, width)
    return (4, 2, 2, width // 16, width * COUNTS[name])


def local(
    inputs,
    encoded,
    target_lengths,
    memory_lengths,
    buckets,
    cotangent,
    self_inward,
    self_outward,
    cross_query,
    cross_reader,
    cross_writer,
    expand_weight,
    shrink_weight,
    norm_gains,
    bias_table,
):
    wide_count = lax.axis_size("wide")
    narrow_count = lax.axis_size("narrow")
    fast = (wide_count, narrow_count) == (16, 2)
    seqs, length, width = inputs.shape
    memory_size = encoded.shape[1]
    rows, mem_rows = seqs * length, seqs * memory_size
    wide_hidden = expand_weight.shape[1] * narrow_count
    shards = dict(
        zip(
            NAMES,
            (
                self_inward,
                self_outward,
                cross_query,
                cross_reader,
                cross_writer,
                expand_weight,
                shrink_weight,
            ),
        )
    )
    hyper = Hyper() if fast else None
    me = hyper.me if fast else jnp.zeros((4,), jnp.int32)

    held = {}
    if fast:
        for first, names in GATHERS:
            packed = jnp.concatenate([cut(name, shards[name], width) for name in names])
            near, near_c, far, far_c = hyper.gather(packed, first)
            start = 0
            for name in names:
                held[name] = Held((near, near_c, far, far_c), first, start)
                start += COUNTS[name]
    else:
        for name in NAMES:
            full = lax.all_gather(shards[name], "narrow", axis=1, tiled=True)
            full = lax.all_gather(full, "wide", axis=0, tiled=True)
            held[name] = Held((full.reshape(whole_shape(name, width)),), "x", 0)

    def grad_outs(name, count):
        if fast:
            block = shape((4, 2, 2, count, width // 16, width // 2), BF)
            return [(block, HB), (block, HB)]
        return [(shape(whole_shape(name, width), BF), HB)]

    dma = pltpu.SemaphoreType.DMA
    x_rows = inputs.reshape(rows, width)
    mem_flat = encoded.reshape(mem_rows, width)
    heads = HEADS
    pairs_count = heads // 2
    turned = buckets.T
    table = jnp.pad(bias_table.T, ((0, 0), (0, 128 - bias_table.shape[0])))

    n1, kept, bias = launch(
        prepare_kernel,
        [(target_lengths, SM), (inputs, VM), (cotangent, VM), (norm_gains, VM), (turned, VM), (table, VM)],
        [
            (shape((rows, width), BF), VM),
            (shape((rows, width), BF), VM),
            (shape((heads, length, length), F32), VM),
        ],
        name="prepare",
    )

    (packed,) = launch(
        functools.partial(inward_kernel, held["inward"]),
        [(me, SM), (n1, VM)] + held["inward"].ins(),
        [(shape((rows, 3 * width), BF), VM)],
        [weight_scratch("inward", width), dma],
        gflop=2.0,
        name="inward",
    )

    bias_spec = pl.BlockSpec((2, length, length), lambda s, p: (p, 0, 0))
    log_spec = pl.BlockSpec((1, 2, length), lambda s, p: (s * pairs_count + p, 0, 0))
    self_mixed, self_log = launch(
        self_forward_kernel,
        [
            (packed, pair_spec(length)),
            (packed, pair_spec(length, pairs_count)),
            (packed, pair_spec(length, 2 * pairs_count)),
            (bias, bias_spec),
        ],
        [
            (shape((rows, width), BF), pair_spec(length)),
            (shape((seqs * pairs_count, 2, length), F32), log_spec),
        ],
        grid=(seqs, pairs_count),
        gflop=3.0,
        name="self_forward",
    )

    (pairs,) = launch(
        functools.partial(memory_kernel, held["reader"]),
        [(me, SM), (memory_lengths, SM), (mem_flat, pl.BlockSpec((KEY_TILE, width), lambda i: (i, 0)))]
        + held["reader"].ins(),
        [(shape((mem_rows, 2 * width), BF), pl.BlockSpec((KEY_TILE, 2 * width), lambda i: (i, 0)))],
        [weight_scratch("reader", width), dma],
        grid=(mem_rows // KEY_TILE,),
        gflop=5.0,
        name="memory",
    )

    after_self, n2, asks = launch(
        functools.partial(middle_kernel, held["outward"], held["query"]),
        [(me, SM), (x_rows, VM), (self_mixed, VM), (norm_gains, VM)]
        + held["outward"].ins()
        + held["query"].ins(),
        [
            (shape((rows, width), F32), VM),
            (shape((rows, width), BF), VM),
            (shape((rows, width), BF), VM),
        ],
        [weight_scratch("outward", width), weight_scratch("query", width), dma((2,))],
        gflop=2.0,
        name="middle",
    )

    cross_mixed, cross_log = launch(
        cross_forward_kernel,
        [
            (memory_lengths, SM),
            (asks, pair_spec(length)),
            (pairs, pair_spec(memory_size)),
            (pairs, pair_spec(memory_size, pairs_count)),
        ],
        [
            (shape((rows, width), BF), pair_spec(length)),
            (shape((seqs * pairs_count, 2, length), F32), log_spec),
        ],
        grid=(seqs, pairs_count),
        gflop=10.0,
        name="cross_forward",
    )

    after_cross, n3, hidden, slope, *shrink_parts = launch(
        functools.partial(widen_kernel, held["writer"], held["expand"]),
        [(me, SM), (after_self, VM), (cross_mixed, VM), (norm_gains, VM), (kept, VM)]
        + held["writer"].ins()
        + held["expand"].ins(),
        [
            (shape((rows, width), F32), VM),
            (shape((rows, width), BF), VM),
            (shape((rows, wide_hidden), BF), VM),
            (shape((rows, wide_hidden), BF), VM),
        ]
        + grad_outs("shrink", 4),
        [
            weight_scratch("writer", width),
            weight_scratch("expand", width),
            weight_scratch("shrink", width),
            dma((3,)),
        ],
        gflop=10.0,
        name="widen",
    )

    layer_out, grad_cross, gain_third, *expand_parts = launch(
        functools.partial(narrow_kernel, held["shrink"], held["expand"]),
        [
            (me, SM),
            (target_lengths, SM),
            (after_cross, VM),
            (n3, VM),
            (hidden, VM),
            (slope, VM),
            (kept, VM),
            (norm_gains, VM),
        ]
        + held["shrink"].ins()
        + held["expand"].ins(),
        [
            (shape((seqs, length, width), BF), VM),
            (shape((rows, width), F32), VM),
            (shape((1, width), F32), VM),
        ]
        + grad_outs("expand", 4),
        [
            weight_scratch("shrink", width),
            weight_scratch("expand", width),
            weight_scratch("expand", width),
            pltpu.VMEM((rows, width), F32),
            pltpu.VMEM((rows, width), F32),
            dma((3,)),
        ],
        gflop=14.0,
        name="narrow",
    )

    grad_mixed, *rest_parts = launch(
        functools.partial(writer_back_kernel, held["writer"]),
        [(me, SM), (grad_cross, VM), (cross_mixed, VM)] + held["writer"].ins(),
        [(shape((rows, width), BF), VM)] + grad_outs("writer", 5),
        [weight_scratch("writer", width), weight_scratch("writer", width), dma((2,))],
        gflop=2.0,
        name="writer_back",
    )
    writer_parts = rest_parts

    grad_asks, grad_mem_keys, grad_mem_values = launch(
        cross_backward_kernel,
        [
            (memory_lengths, SM),
            (asks, pair_spec(length)),
            (pairs, pair_spec(memory_size)),
            (pairs, pair_spec(memory_size, pairs_count)),
            (grad_mixed, pair_spec(length)),
            (cross_log, log_spec),
        ],
        [
            (shape((rows, width), BF), pair_spec(length)),
            (shape((mem_rows, width), BF), pair_spec(memory_size)),
            (shape((mem_rows, width), BF), pair_spec(memory_size)),
        ],
        grid=(seqs, pairs_count),
        gflop=20.0,
        name="cross_backward",
    )

    tile_spec = pl.BlockSpec((KEY_TILE, width), lambda i: (i, 0))
    into = [(a, HB) for a in rest_parts] if fast else []
    rest_parts = launch(
        functools.partial(reader_grad_kernel, fast),
        [
            (me, SM),
            (memory_lengths, SM),
            (mem_flat, tile_spec),
            (grad_mem_keys, tile_spec),
            (grad_mem_values, tile_spec),
        ]
        + into,
        grad_outs("reader", 5),
        [weight_scratch("reader", width), pltpu.VMEM((width, 2 * width), F32), dma],
        grid=(mem_rows // KEY_TILE,),
        alias={5: 0, 6: 1} if fast else None,
        gflop=5.0,
        name="reader_grad",
    )
    reader_parts = rest_parts

    into = [(a, HB) for a in rest_parts] if fast else []
    base = 7 + 2 * len(held["query"].arrays)
    grad_self, grad_mixed, gain_second, *rest_parts = launch(
        functools.partial(query_back_kernel, fast, held["query"], held["outward"]),
        [
            (me, SM),
            (grad_asks, VM),
            (n2, VM),
            (after_self, VM),
            (grad_cross, VM),
            (self_mixed, VM),
            (norm_gains, VM),
        ]
        + held["query"].ins()
        + held["outward"].ins()
        + into,
        [
            (shape((rows, width), F32), VM),
            (shape((rows, width), BF), VM),
            (shape((1, width), F32), VM),
        ]
        + (grad_outs("query", 5) if fast else grad_outs("query", 1) + grad_outs("outward", 1)),
        [
            weight_scratch("query", width),
            weight_scratch("outward", width),
            weight_scratch("query", width),
            weight_scratch("outward", width),
            dma((4,)),
        ],
        alias={base: 3, base + 1: 4} if fast else None,
        gflop=3.0,
        name="query_back",
    )

    bias_flip = pl.BlockSpec((2, length, length), lambda p, s: (p, 0, 0))
    log_flip = pl.BlockSpec((1, 2, length), lambda p, s: (s * pairs_count + p, 0, 0))
    grad_query, grad_keys, grad_values, grad_bias = launch(
        self_backward_kernel,
        [
            (packed, pair_spec(length, 0, True)),
            (packed, pair_spec(length, pairs_count, True)),
            (packed, pair_spec(length, 2 * pairs_count, True)),
            (grad_mixed, pair_spec(length, 0, True)),
            (bias, bias_flip),
            (self_log, log_flip),
        ],
        [(shape((rows, width), BF), pair_spec(length, 0, True))] * 3
        + [(shape((heads, length, length), F32), bias_flip)],
        grid=(pairs_count, seqs),
        gflop=6.0,
        name="self_backward",
    )

    inward_parts = launch(
        inward_grad_kernel,
        [(me, SM), (n1, VM), (grad_query, VM), (grad_keys, VM), (grad_values, VM)],
        grad_outs("inward", 3),
        [weight_scratch("inward", width), dma],
        gflop=2.0,
        name="inward_grad",
    )

    inputs_grad, gain_first = launch(
        functools.partial(inputs_grad_kernel, held["inward"]),
        [
            (me, SM),
            (x_rows, VM),
            (grad_query, VM),
            (grad_keys, VM),
            (grad_values, VM),
            (grad_self, VM),
            (norm_gains, VM),
        ]
        + held["inward"].ins(),
        [(shape((rows, width), F32), VM), (shape((1, width), F32), VM)],
        [weight_scratch("inward", width), dma],
        gflop=2.0,
        name="inputs_grad",
    )

    (encoded_grad,) = launch(
        functools.partial(encoded_grad_kernel, held["reader"]),
        [(me, SM), (memory_lengths, SM), (grad_mem_keys, tile_spec), (grad_mem_values, tile_spec)]
        + held["reader"].ins(),
        [(shape((mem_rows, width), F32), tile_spec)],
        [weight_scratch("reader", width), dma],
        grid=(mem_rows // KEY_TILE,),
        gflop=5.0,
        name="encoded_grad",
    )

    (table_part,) = launch(
        table_kernel,
        [(turned, VM), (grad_bias, VM)],
        [(shape((bias_table.shape[0], heads, length), F32), VM)],
        gflop=3.0,
        name="table",
    )
    table_part = jnp.sum(table_part, axis=-1)
    gains_part = jnp.concatenate((gain_first, gain_second, gain_third))

    sums = {}
    if fast:
        chunks = (
            (shrink_parts, "x", ("shrink",)),
            (expand_parts, "y", ("expand",)),
            (rest_parts, "x", ("writer", "query", "outward", "reader")),
            (inward_parts, "y", ("inward",)),
        )
        for (keep, send), first, names in chunks:
            pieces = hyper.scatter(keep, send, first)
            start = 0
            for name in names:
                sums[name] = uncut(name, pieces[start : start + COUNTS[name]])
                start += COUNTS[name]
    else:
        parts = {
            "shrink": shrink_parts[0],
            "expand": expand_parts[0],
            "writer": writer_parts[0],
            "reader": reader_parts[0],
            "query": rest_parts[0],
            "outward": rest_parts[1],
            "inward": inward_parts[0],
        }
        for name in NAMES:
            full = parts[name].reshape(-1, parts[name].shape[-1]).astype(F32)
            full = lax.psum_scatter(full, "wide", scatter_dimension=0, tiled=True)
            sums[name] = lax.psum_scatter(full, "narrow", scatter_dimension=1, tiled=True)

    row_parts = [jnp.sum(sums[name] * sums[name], axis=1) for name in NAMES]
    col_parts = [jnp.sum(sums[name] * sums[name], axis=0) for name in NAMES]
    totals = jnp.stack([jnp.sum(part) for part in row_parts])
    shared = jnp.concatenate((totals, gains_part.reshape(-1), table_part.reshape(-1)))
    row_sizes = [part.shape[0] for part in row_parts]
    col_sizes = [part.shape[0] for part in col_parts]
    first_sum = jnp.concatenate(row_parts + [shared])
    if fast:
        first_sum = hyper.total(first_sum, ("y",))
    else:
        first_sum = lax.psum(first_sum, "narrow")
    second_sum = jnp.concatenate(col_parts + [first_sum[sum(row_sizes) :]])
    if fast:
        second_sum = hyper.total(second_sum, ("c", "x", "z1", "z2"))
    else:
        second_sum = lax.psum(second_sum, "wide")

    results = []
    row_at = col_at = 0
    tail = sum(col_sizes)
    for index, name in enumerate(NAMES):
        grad = sums[name]
        full_rows = grad.shape[0] * wide_count
        full_cols = grad.shape[1] * narrow_count
        row_stat = first_sum[row_at : row_at + row_sizes[index]] / full_cols + TINY
        col_stat = second_sum[col_at : col_at + col_sizes[index]] / full_rows + TINY
        row_at += row_sizes[index]
        col_at += col_sizes[index]
        mean_rows = second_sum[tail + index] / (full_rows * full_cols) + TINY
        step = grad * lax.rsqrt(row_stat[:, None] * col_stat[None, :] / mean_rows)
        results.extend([grad, step, row_stat, col_stat])
    gains_grad = second_sum[tail + 7 : tail + 7 + gains_part.size].reshape(gains_part.shape)
    table_grad = second_sum[tail + 7 + gains_part.size :].reshape(table_part.shape)
    return (
        (
            layer_out,
            inputs_grad.reshape(inputs.shape),
            encoded_grad.reshape(encoded.shape),
        )
        + tuple(results)
        + (gains_grad, table_grad)
    )


def solution(mesh):
    tokens = P(BOTH, None, None)
    weight = P("wide", "narrow")
    per_weight = (weight, weight, P("wide"), P("narrow"))
    return jax.shard_map(
        local,
        mesh=mesh,
        in_specs=(tokens, tokens, P(BOTH), P(BOTH), P(), tokens) + (weight,) * 7 + (P(), P()),
        out_specs=(tokens, tokens, tokens) + per_weight * 7 + (P(), P()),
        check_vma=False,
    )
```

time: 1300 us -> 535 us (0.41); the launches traced: 1280 us -> 531 us
  matrix products: 416 us -> 0 us
  waiting for transfers between devices: 407 us -> 179 us
  Pallas kernels: 0 us -> 207 us
  local copies, waits for them, and re-layouts: 220 us -> 26.8 us
  blocking collectives: 151 us -> 0 us
  starting transfers between devices: 0.86 us -> 57.1 us
  between operations: 20 us -> 6.25 us
    dot_general x191 -> x0, matrix products: 416 us -> none  [the longest x48 69.5 us: head_scores(): jnp.einsum('sqd,skd->sqk', query, keys, preferred_element_type=jnp.float32)]
    reduce_scatter x13 -> x0, waiting for transfers between devices: 334 us -> none  [the longest x1 105 us: settle(): lax.psum_scatter(seventh, 'wide', scatter_dimension=0, tiled=True)]
    pallas_call x0 -> x17, Pallas kernels: none -> 207 us  [launch(): pl.pallas_call(body, grid=grid if grid is not None else (), in_specs=[s f...]
    ppermute x0 -> x49, waiting for transfers between devices: none -> 179 us  [swap(): return lax.ppermute(value, BOTH, [(i, i ^ mask) for i in range(32)])]
    psum x3 -> x0, blocking collectives: 106 us -> none  [the longest x1 60.6 us: local(): lax.psum((col_parts[0], col_parts[1], col_parts[2], col_parts[3], col_par...]
    dynamic_update_slice x24 -> x0, local copies, waits for them, and re-layouts: 95.1 us -> none  [attend_backward(): return lax.map(one_head, (query, keys, values, extra, logsum, grad_mixed))]
    all_gather x7 -> x0, waiting for transfers between devices: 71.3 us -> none  [the longest x1 28.6 us: fetch(): lax.all_gather(seventh, 'wide', axis=0, tiled=True)]
    ppermute x0 -> x49, starting transfers between devices: none -> 57.1 us  [swap(): return lax.ppermute(value, BOTH, [(i, i ^ mask) for i in range(32)])]
  transfers between devices with their start and end apart: 21 -> 49, of which waited for: 11 -> 19; matrix products, arithmetic and copies ran while one was open for 41% -> 11% of each run, Pallas kernels for 0% -> 26%
where the time goes in v1:
time: 535 us; the launch traced here: 531 us
  Pallas kernels  207 us (39%)
  waiting for transfers between devices  179 us (33%)
  starting transfers between devices  57.1 us (11%)
  other arithmetic  55.9 us (10%)
  local copies, waits for them, and re-layouts  26.8 us (5%)
  between operations  6.25 us (1%)
    pallas_call x17, Pallas kernels, launch(): pl.pallas_call(body, grid=grid if grid is not None else (), in_specs=[s f...  207 us
    ppermute x49, waiting for transfers between devices, swap(): return lax.ppermute(value, BOTH, [(i, i ^ mask) for i in range(32)])  179 us
    ppermute x49, starting transfers between devices, swap(): return lax.ppermute(value, BOTH, [(i, i ^ mask) for i in range(32)])  57.1 us
    unnamed x100, local copies, waits for them, and re-layouts  14.5 us
    convert_element_type x4, other arithmetic, scatter(): sent = add(lambda p: pick(p, 1 - where[first])).astype(BF)  11.1 us
  transfers between devices with their start and end apart: 49, of which 19 were waited for; matrix products, arithmetic and copies ran while one was open for 11% of the time, Pallas kernels for 26%

profile of v1, /device:TPU:0, one launch (start us, length us, event | category | flops | bytes accessed | tf_op | source)
XLA Modules:
  0.0 531.3 jit_solution(7585900869299881018)
XLA Ops:
  2.5 3.1 collective-permute-start
  5.6 4.6 collective-permute-done
  10.3 2.8 collective-permute-start.1
  13.2 15.8 %collective-permute-done.1 = bf16[2,5,48,384]{3,2,1,0:T(8,128)(2,1)S(1)} collective-permute-done((bf16[2,5,48,384]{3,2,1,0:T(8,128)(2,1)S(1)}, bf16[2,5,48,384]{3,2,1,0:T(8,128)(2,1)S(1)}, u32[]{:S(2)}, u32[]{:S(2)}) %collective-permute-start.1) | collective-permute-done | bytes 368672 | tf_op jit(solution)/shard_map/ppermute | solution.py:570
  33.4 3.1 collective-permute-done.6
  36.6 2.1 collective-permute-start.7
  38.9 7.8 %collective-permute-done.2 = bf16[4,5,48,384]{3,2,1,0:T(8,128)(2,1)S(1)} collective-permute-done((bf16[4,5,48,384]{3,2,1,0:T(8,128)(2,1)S(1)}, bf16[4,5,48,384]{3,2,1,0:T(8,128)(2,1)S(1)}, u32[]{:S(2)}, u32[]{:S(2)}) %collective-permute-start.2) | collective-permute-done | bytes 737312 | tf_op jit(solution)/shard_map/ppermute | solution.py:570
  48.4 1.6 collective-permute-start.8
  50.2 3.0 collective-permute-start.19
  53.2 35.5 %collective-permute-done.8 = bf16[4,3,48,384]{3,2,1,0:T(8,128)(2,1)S(1)} collective-permute-done((bf16[4,3,48,384]{3,2,1,0:T(8,128)(2,1)S(1)}, bf16[4,3,48,384]{3,2,1,0:T(8,128)(2,1)S(1)}, u32[]{:S(2)}, u32[]{:S(2)}) %collective-permute-start.8) | collective-permute-done | bytes 442400 | tf_op jit(solution)/shard_map/ppermute | solution.py:570
  92.6 27.8 %collective-permute-done.14 = bf16[4,4,48,384]{3,2,1,0:T(8,128)(2,1)S(1)} collective-permute-done((bf16[4,4,48,384]{3,2,1,0:T(8,128)(2,1)S(1)}, bf16[4,4,48,384]{3,2,1,0:T(8,128)(2,1)S(1)}, u32[]{:S(2)}, u32[]{:S(2)}) %collective-permute-start.14) | collective-permute-done | bytes 589856 | tf_op jit(solution)/shard_map/ppermute | solution.py:570
  128.5 7.4 %prepare.1 = (bf16[512,768]{1,0:T(8,128)(2,1)}, bf16[512,768]{1,0:T(8,128)(2,1)}, f32[12,256,256]{2,1,0:T(8,128)}) custom-call(s32[2]{0:T(128)} %lens.10, bf16[2,256,768]{2,1,0:T(8,128)(2,1)} %x.3, bf16[2,256,768]{2,1,0:T(8,128)(2,1)} %cot.1, f32[3,768]{1,0:T(4,128)} %gains.11, s32[256,256]{1,0:T(8,128)} %bitcast.161, f32[12,128]{1,0:T(8,128)} %pad.4.table), custom_call_target="tpu_custom_call" | custom-call | flops 1000000000 | bytes 4194304 | tf_op jit(solution)/shard_map/prepare/pallas_call | solution.py:60
  136.5 10.9 %memory.1.keys.values = bf16[2048,1536]{1,0:T(8,128)(2,1)} custom-call(s32[4]{0:T(128)} %pad_add_fusion.me, s32[2]{0:T(128)} %lens.13, bf16[2048,768]{1,0:T(8,128)(2,1)} %bitcast.170, bf16[2,4,3,48,384]{4,3,2,1,0:T(8,128)(2,1)} %copy-done.8, bf16[2,4,3,48,384]{4,3,2,1,0:T(8,128)(2,1)} %copy-done.44, ...), custom_call_target="tpu_custom_call" | custom-call | flops 5000000000 | bytes 4194304 | tf_op jit(solution)/shard_map/memory/pallas_call | solution.py:60
  147.4 3.7 collective-permute-done.16.rest_6_
  151.1 2.8 collective-permute-done.22.rest_2_
  154.4 6.7 %inward.1.query.keys.values = bf16[512,2304]{1,0:T(8,128)(2,1)} custom-call(s32[4]{0:T(128)} %pad_add_fusion.me, bf16[512,768]{1,0:T(8,128)(2,1)} %get-tuple-element.75.n1, bf16[2,4,5,48,384]{4,3,2,1,0:T(8,128)(2,1)} %copy-done, bf16[2,4,5,48,384]{4,3,2,1,0:T(8,128)(2,1)} %collective-permute-done.3.rest_1_.rest_5_, bf16[2,4,5,48,384]{4,3,2,1,0:T(8,128)(2,1)} %copy-done.1, ...), custom_call_target="tpu_custom_call" | custom-call | flops 2000000000 | bytes 4194304 | tf_op jit(solution)/shard_map/inward/pallas_call | solution.py:60
  161.1 13.5 %self_forward.1 = (bf16[512,768]{1,0:T(8,128)(2,1)}, f32[12,2,256]{2,1,0:T(2,128)}) custom-call(bf16[512,2304]{1,0:T(8,128)(2,1)} %inward.1.query.keys.values, bf16[512,2304]{1,0:T(8,128)(2,1)} %inward.1.query.keys.values, bf16[512,2304]{1,0:T(8,128)(2,1)} %inward.1.query.keys.values, f32[12,256,256]{2,1,0:T(8,128)} %get-tuple-element.76.bias), custom_call_target="tpu_custom_call" | custom-call | flops 3000000000 | bytes 4194304 | tf_op jit(solution)/shard_map/self_forward/pallas_call | solution.py:60
  174.6 5.8 %middle.1 = (f32[512,768]{1,0:T(8,128)}, bf16[512,768]{1,0:T(8,128)(2,1)}, bf16[512,768]{1,0:T(8,128)(2,1)}) custom-call(s32[4]{0:T(128)} %pad_add_fusion.me, bf16[512,768]{1,0:T(8,128)(2,1)} %bitcast.126, bf16[512,768]{1,0:T(8,128)(2,1)} %get-tuple-element.77.mixed, f32[3,768]{1,0:T(4,128)} %gains.11, bf16[2,4,5,48,384]{4,3,2,1,0:T(8,128)(2,1)} %copy-done, ...), custom_call_target="tpu_custom_call" | custom-call | flops 2000000000 | bytes 4194304 | tf_op jit(solution)/shard_map/middle/pallas_call | solution.py:60
  180.3 19.9 %cross_forward.1 = (bf16[512,768]{1,0:T(8,128)(2,1)}, f32[12,2,256]{2,1,0:T(2,128)}) custom-call(s32[2]{0:T(128)} %lens.13, bf16[512,768]{1,0:T(8,128)(2,1)} %get-tuple-element.79.query, bf16[2048,1536]{1,0:T(8,128)(2,1)} %memory.1.keys.values, bf16[2048,1536]{1,0:T(8,128)(2,1)} %memory.1.keys.values), custom_call_target="tpu_custom_call" | custom-call | flops 10000000000 | bytes 4194304 | tf_op jit(solution)/shard_map/cross_forward/pallas_call | solution.py:60
  201.6 18.0 %widen.1 = (f32[512,768]{1,0:T(8,128)}, bf16[512,768]{1,0:T(8,128)(2,1)}, bf16[512,3072]{1,0:T(8,128)(2,1)}, bf16[512,3072]{1,0:T(8,128)(2,1)}, bf16[4,2,2,4,48,...) custom-call(s32[4]{0:T(128)} %pad_add_fusion.me, f32[512,768]{1,0:T(8,128)} %get-tuple-element.78.after_self, ...), custom_call_target="tpu_custom_call" | custom-call | flops 10000000000 | bytes 4194304 | tf_op jit(solution)/shard_map/widen/pallas_call | solution.py:60
  221.0 22.3 %narrow.1 = (bf16[2,256,768]{2,1,0:T(8,128)(2,1)}, f32[512,768]{1,0:T(8,128)}, f32[1,768]{1,0:T(1,128)}, bf16[4,2,2,4,48,384]{5,4,3,2,1,0:T(8,128)(2,1)}, bf16[4,2,2,4,48,384]{5,4,3,2,1,0:T(8,128)(2,1)}) custom-call(s32[4]{0:T(128)} %pad_add_fusion.me, s32[2]{0:T(128)} %lens.10, f32[512,768]{1,0:T(8,128)} %get-tuple-element.82.after_cross, ...), custom_call_target="tpu_custom_call" | custom-call | flops 14000000000 | bytes 4194304 | tf_op jit(solution)/shard_map/narrow/pallas_call | solution.py:60
  243.3 4.9 writer_back.1
  248.2 23.3 %cross_backward.1 = (bf16[512,768]{1,0:T(8,128)(2,1)}, bf16[2048,768]{1,0:T(8,128)(2,1)}, bf16[2048,768]{1,0:T(8,128)(2,1)}) custom-call(s32[2]{0:T(128)} %lens.13, bf16[512,768]{1,0:T(8,128)(2,1)} %get-tuple-element.79.query, bf16[2048,1536]{1,0:T(8,128)(2,1)} %memory.1.keys.values, bf16[2048,1536]{1,0:T(8,128)(2,1)} %memory.1.keys.values, ...), custom_call_target="tpu_custom_call" | custom-call | flops 20000000000 | bytes 4194304 | tf_op jit(solution)/shard_map/cross_backward/pallas_call | solution.py:60
  271.5 10.9 %reader_grad.1 = (bf16[4,2,2,5,48,384]{5,4,3,2,1,0:T(8,128)(2,1)}, bf16[4,2,2,5,48,384]{5,4,3,2,1,0:T(8,128)(2,1)}) custom-call(s32[4]{0:T(128)} %pad_add_fusion.me, s32[2]{0:T(128)} %lens.13, bf16[2048,768]{1,0:T(8,128)(2,1)} %bitcast.171, bf16[2048,768]{1,0:T(8,128)(2,1)} %get-tuple-element.92.gk, ...), custom_call_target="tpu_custom_call", output_to_operand_aliasing={{0}: (5, {}), {1}: (6, {})} | custom-call | flops 5000000000 | bytes 4194304 | tf_op jit(solution)/shard_map/reader_grad/pallas_call | solution.py:60
  282.3 9.3 %query_back.1 = (f32[512,768]{1,0:T(8,128)}, bf16[512,768]{1,0:T(8,128)(2,1)}, f32[1,768]{1,0:T(1,128)}, bf16[4,2,2,5,48,384]{5,4,3,2,1,0:T(8,128)(2,1)}, bf16[4,2,2,5,48,384]{5,4,3,2,1,0:T(8,128)(2,1)}) custom-call(s32[4]{0:T(128)} %pad_add_fusion.me, bf16[512,768]{1,0:T(8,128)(2,1)} %get-tuple-element.90.grad_asks, ...), custom_call_target="tpu_custom_call", output_to_operand_aliasing={{3}: (15, {}), {4}: (16, {})} | custom-call | flops 3000000000 | bytes 4194304 | tf_op jit(solution)/shard_map/query_back/pallas_call | solution.py:60
  292.3 14.5 %self_backward.1 = (bf16[512,768]{1,0:T(8,128)(2,1)}, bf16[512,768]{1,0:T(8,128)(2,1)}, bf16[512,768]{1,0:T(8,128)(2,1)}, f32[12,256,256]{2,1,0:T(8,128)}) custom-call(bf16[512,2304]{1,0:T(8,128)(2,1)} %inward.1.query.keys.values, bf16[512,2304]{1,0:T(8,128)(2,1)} %inward.1.query.keys.values, bf16[512,2304]{1,0:T(8,128)(2,1)} %inward.1.query.keys.values, ...), custom_call_target="tpu_custom_call" | custom-call | flops 6000000000 | bytes 4194304 | tf_op jit(solution)/shard_map/self_backward/pallas_call | solution.py:60
  306.8 5.8 %inward_grad.1 = (bf16[4,2,2,3,48,384]{5,4,3,2,1,0:T(8,128)(2,1)}, bf16[4,2,2,3,48,384]{5,4,3,2,1,0:T(8,128)(2,1)}) custom-call(s32[4]{0:T(128)} %pad_add_fusion.me, bf16[512,768]{1,0:T(8,128)(2,1)} %get-tuple-element.75.n1, bf16[512,768]{1,0:T(8,128)(2,1)} %get-tuple-element.100.gq, bf16[512,768]{1,0:T(8,128)(2,1)} %get-tuple-element.101.gk, ...), custom_call_target="tpu_custom_call" | custom-call | flops 2000000000 | bytes 4194304 | tf_op jit(solution)/shard_map/inward_grad/pallas_call | solution.py:60
  313.2 3.7 collective-permute-done.24
  316.8 2.6 add_convert_fusion.3
  319.5 3.1 add_convert_fusion
  322.6 6.0 %collective-permute-start.30 = (bf16[4,1,2,5,48,384]{5,4,3,2,1,0:T(8,128)(2,1)}, bf16[4,1,2,5,48,384]{5,4,3,2,1,0:T(8,128)(2,1)}, u32[]{:S(2)}, u32[]{:S(2)}) collective-permute-start(bf16[4,1,2,5,48,384]{5,4,3,2,1,0:T(8,128)(2,1)} %add_convert_fusion), channel_id=1, source_target_pairs={{0,4},{1,5},{2,6},{3,7},{4,0},{5,1},{6,2},{7,3},{8,12},{9,13},{10,... | collective-permute-start | bytes 4423688 | tf_op jit(solution)/shard_map/ppermute | solution.py:570
  328.6 2.8 add_convert_fusion.1
  331.3 2.6 add_convert_fusion.2
  334.0 2.0 collective-permute-start.35
  336.0 8.1 %inputs_grad.1 = (f32[512,768]{1,0:T(8,128)}, f32[1,768]{1,0:T(1,128)}) custom-call(s32[4]{0:T(128)} %pad_add_fusion.me, bf16[512,768]{1,0:T(8,128)(2,1)} %bitcast.127, bf16[512,768]{1,0:T(8,128)(2,1)} %get-tuple-element.100.gq, bf16[512,768]{1,0:T(8,128)(2,1)} %get-tuple-element.101.gk, bf16[512,768]{1,0:T(8,128)(2,1)} %get-tuple-element.102.gv, ...), custom_call_target="tpu_custom_call" | custom-call | flops 2000000000 | bytes 4194304 | tf_op jit(solution)/shard_map/inputs_grad/pallas_call | solution.py:60
  344.1 2.2 add_convert_fusion.7
  346.3 4.1 collective-permute-start.26
  351.1 36.1 %collective-permute-done.40 = bf16[4,1,2,4,48,384]{5,4,3,2,1,0:T(8,128)(2,1)} collective-permute-done((bf16[4,1,2,4,48,384]{5,4,3,2,1,0:T(8,128)(2,1)}, bf16[4,1,2,4,48,384]{5,4,3,2,1,0:T(8,128)(2,1)}, u32[]{:S(2)}, u32[]{:S(2)}) %collective-permute-start.40) | collective-permute-done | bytes 1179680 | tf_op jit(solution)/shard_map/ppermute | solution.py:570
  387.2 2.4 add_convert_fusion.5
  389.7 2.0 collective-permute-start.41
  391.7 2.5 add_convert_fusion.6
  394.2 2.1 collective-permute-start.36
  396.2 2.5 add_convert_fusion.4
  398.8 2.1 add_convert_fusion.11
  400.9 13.8 %table.1 = f32[32,12,256]{2,1,0:T(8,128)} custom-call(s32[256,256]{1,0:T(8,128)} %bitcast.162, f32[12,256,256]{2,1,0:T(8,128)} %get-tuple-element.116.grad_bias), custom_call_target="tpu_custom_call" | custom-call | flops 3000000000 | bytes 4194304 | tf_op jit(solution)/shard_map/table/pallas_call | solution.py:60
  417.8 4.1 collective-permute-start.28
  421.9 2.1 add_convert_fusion.9
  424.0 2.9 collective-permute-start.42
  426.9 2.2 add_convert_fusion.10
  429.2 2.1 add_convert_fusion.8
  431.3 2.9 collective-permute-start.32
  434.2 1.9 fusion.4
  437.4 15.6 %collective-permute-done.42 = bf16[2,1,1,4,48,384]{5,4,3,2,1,0:T(8,128)(2,1)} collective-permute-done((bf16[2,1,1,4,48,384]{5,4,3,2,1,0:T(8,128)(2,1)}, bf16[2,1,1,4,48,384]{5,4,3,2,1,0:T(8,128)(2,1)}, u32[]{:S(2)}, u32[]{:S(2)}) %collective-permute-start.42) | collective-permute-done | bytes 294944 | tf_op jit(solution)/shard_map/ppermute | solution.py:570
  454.4 5.0 collective-permute-done.37
  460.8 5.3 collective-permute-done.32
  467.5 1.6 collective-permute-done.43
  469.1 2.6 multiply_reduce_fusion.1
  472.4 2.7 fusion.1
  478.9 5.3 %concatenate.226 = f32[3175]{0:T(1024)S(1)} concatenate(f32[48]{0:T(128)} %get-tuple-element.161, f32[48]{0:T(128)S(1)} %get-tuple-element.181, f32[48]{0:T(128)S(1)} %get-tuple-element.177, f32[48]{0:T(128)S(1)} %get-tuple-element.152, f32[48]{0:T(128)S(1)} %get-tuple-element.164, f32[48]{0:T(128)} %get-tuple-element.158, f32[192]{0:T(256)} %reduce_sum.213, f32[1]{0:T(128)} %bitcast.48, ...), dimensions={0} | concatenate | bytes 25400 | tf_op jit(solution)/shard_map/concatenate | solution.py:1035
  495.0 11.6 %encoded_grad.1 = f32[2048,768]{1,0:T(8,128)} custom-call(s32[4]{0:T(128)} %pad_add_fusion.me, s32[2]{0:T(128)} %lens.13, bf16[2048,768]{1,0:T(8,128)(2,1)} %get-tuple-element.92.gk, bf16[2048,768]{1,0:T(8,128)(2,1)} %get-tuple-element.93.gv, bf16[2,4,3,48,384]{4,3,2,1,0:T(8,128)(2,1)} %copy-done.8, bf16[2,4,3,48,384]{4,3,2,1,0:T(8,128)(2,1)} %copy-done.44, ...), custom_call_target="tpu_custom_call" | custom-call | flops 5000000000 | bytes 4194304 | tf_op jit(solution)/shard_map/encoded_grad/pallas_call | solution.py:60
  508.2 2.5 collective-permute-done.46
  510.9 3.8 collective-permute-done.47
  514.7 1.6 collective-permute-start.48
  516.3 3.2 collective-permute-done.48
  (235 shorter events, 58.4 us)
Async XLA Ops:
  0.7 29.8 %copy-start.18 = (bf16[48,768]{1,0:T(8,128)(2,1)S(1)}, bf16[48,768]{1,0:T(8,128)(2,1)}, u32[]{:S(2)}) copy-start(bf16[48,768]{1,0:T(8,128)(2,1)} %param.24) | copy-start | bytes 221188
  0.7 29.9 %copy-start.20 = (bf16[48,384]{1,0:T(8,128)(2,1)S(1)}, bf16[48,384]{1,0:T(8,128)(2,1)}, u32[]{:S(2)}) copy-start(bf16[48,384]{1,0:T(8,128)(2,1)} %param.25) | copy-start | bytes 110596
  0.7 30.6 %copy-start.17 = (bf16[48,1536]{1,0:T(8,128)(2,1)S(1)}, bf16[48,1536]{1,0:T(8,128)(2,1)}, u32[]{:S(2)}) copy-start(bf16[48,1536]{1,0:T(8,128)(2,1)} %param.26) | copy-start | bytes 442372
  1.7 31.1 %copy-start.12 = (bf16[192,384]{1,0:T(8,128)(2,1)S(1)}, bf16[192,384]{1,0:T(8,128)(2,1)}, u32[]{:S(2)}) copy-start(bf16[192,384]{1,0:T(8,128)(2,1)} %param.27) | copy-start | bytes 442372
  2.5 7.7 %collective-permute-start = (bf16[5,48,384]{2,1,0:T(8,128)(2,1)S(1)}, bf16[5,48,384]{2,1,0:T(8,128)(2,1)S(1)}, u32[]{:S(2)}, u32[]{:S(2)}) collective-permute-start(bf16[5,48,384]{2,1,0:T(8,128)(2,1)S(1)} %get-tuple-element.186), channel_id=1, source_target_pairs={{0,8},{1,9},{2,10},{3,11},{4,12},{5,13},{6,14},{7,15},{8,0},{9,1},... | collective-permute-start | bytes 552968 | tf_op jit(solution)/shard_map/ppermute | solution.py:570
  10.3 18.6 %collective-permute-start.1 = (bf16[2,5,48,384]{3,2,1,0:T(8,128)(2,1)S(1)}, bf16[2,5,48,384]{3,2,1,0:T(8,128)(2,1)S(1)}, u32[]{:S(2)}, u32[]{:S(2)}) collective-permute-start(bf16[2,5,48,384]{3,2,1,0:T(8,128)(2,1)S(1)} %maximum_select_fusion.8), channel_id=1, source_target_pairs={{0,16},{1,17},{2,18},{3,19},{4,20},{5,21},{6,22},{7,23},{8,24},{9,... | collective-permute-start | bytes 1105928 | tf_op jit(solution)/shard_map/ppermute | solution.py:570
  29.1 17.5 %collective-permute-start.2 = (bf16[4,5,48,384]{3,2,1,0:T(8,128)(2,1)S(1)}, bf16[4,5,48,384]{3,2,1,0:T(8,128)(2,1)S(1)}, u32[]{:S(2)}, u32[]{:S(2)}) collective-permute-start(bf16[4,5,48,384]{3,2,1,0:T(8,128)(2,1)S(1)} %maximum_select_fusion.1), channel_id=1, source_target_pairs={{0,4},{1,5},{2,6},{3,7},{4,0},{5,1},{6,2},{7,3},{8,12},{9,13},{10,... | collective-permute-start | bytes 2211848 | tf_op jit(solution)/shard_map/ppermute | solution.py:570
  30.6 6.0 %collective-permute-start.6 = (bf16[3,48,384]{2,1,0:T(8,128)(2,1)S(1)}, bf16[3,48,384]{2,1,0:T(8,128)(2,1)S(1)}, u32[]{:S(2)}, u32[]{:S(2)}) collective-permute-start(bf16[3,48,384]{2,1,0:T(8,128)(2,1)S(1)} %get-tuple-element.190), channel_id=1, source_target_pairs={{0,8},{1,9},{2,10},{3,11},{4,12},{5,13},{6,14},{7,15},{8,0},{9,1},... | collective-permute-start | bytes 331784 | tf_op jit(solution)/shard_map/ppermute | solution.py:570
  31.3 18.6 %collective-permute-start.12 = (bf16[4,48,384]{2,1,0:T(8,128)(2,1)S(1)}, bf16[4,48,384]{2,1,0:T(8,128)(2,1)S(1)}, u32[]{:S(2)}, u32[]{:S(2)}) collective-permute-start(bf16[4,48,384]{2,1,0:T(8,128)(2,1)S(1)} %bitcast.129), channel_id=1, source_target_pairs={{0,8},{1,9},{2,10},{3,11},{4,12},{5,13},{6,14},{7,15},{8,0},{9,1},... | collective-permute-start | bytes 442376 | tf_op jit(solution)/shard_map/ppermute | solution.py:570
  32.8 17.4 %collective-permute-start.18 = (bf16[4,48,384]{2,1,0:T(8,128)(2,1)S(1)}, bf16[4,48,384]{2,1,0:T(8,128)(2,1)S(1)}, u32[]{:S(2)}, u32[]{:S(2)}) collective-permute-start(bf16[4,48,384]{2,1,0:T(8,128)(2,1)S(1)} %bitcast.149), channel_id=1, source_target_pairs={{0,8},{1,9},{2,10},{3,11},{4,12},{5,13},{6,14},{7,15},{8,0},{9,1},... | collective-permute-start | bytes 442376 | tf_op jit(solution)/shard_map/ppermute | solution.py:570
  36.6 11.7 %collective-permute-start.7 = (bf16[2,3,48,384]{3,2,1,0:T(8,128)(2,1)S(1)}, bf16[2,3,48,384]{3,2,1,0:T(8,128)(2,1)S(1)}, u32[]{:S(2)}, u32[]{:S(2)}) collective-permute-start(bf16[2,3,48,384]{3,2,1,0:T(8,128)(2,1)S(1)} %maximum_select_fusion.11), channel_id=1, source_target_pairs={{0,16},{1,17},{2,18},{3,19},{4,20},{5,21},{6,22},{7,23},{8,24},{9,... | collective-permute-start | bytes 663560 | tf_op jit(solution)/shard_map/ppermute | solution.py:570
  46.8 73.5 %copy-start = (bf16[2,4,5,48,384]{4,3,2,1,0:T(8,128)(2,1)}, bf16[2,4,5,48,384]{4,3,2,1,0:T(8,128)(2,1)S(1)}, u32[]{:S(2)}) copy-start(bf16[2,4,5,48,384]{4,3,2,1,0:T(8,128)(2,1)S(1)} %pad_maximum_fusion.rest_0_.rest_4_) | copy-start | bytes 4423684
  46.9 73.5 %collective-permute-start.4 = (bf16[2,4,5,48,384]{4,3,2,1,0:T(8,128)(2,1)S(1)}, bf16[2,4,5,48,384]{4,3,2,1,0:T(8,128)(2,1)S(1)}, u32[]{:S(2)}, u32[]{:S(2)}) collective-permute-start(bf16[2,4,5,48,384]{4,3,2,1,0:T(8,128)(2,1)S(1)} %pad_maximum_fusion.rest_0_.rest_4_), channel_id=1, source_target_pairs={{0,1},{1,0},{2,3},{3,2},{4,5},{5,4},{6,7},{7,6},{8,9},{9,8},{10,11... | collective-permute-start | bytes 4423688 | tf_op jit(solution)/shard_map/ppermute | solution.py:570
  48.4 40.4 %collective-permute-start.8 = (bf16[4,3,48,384]{3,2,1,0:T(8,128)(2,1)S(1)}, bf16[4,3,48,384]{3,2,1,0:T(8,128)(2,1)S(1)}, u32[]{:S(2)}, u32[]{:S(2)}) collective-permute-start(bf16[4,3,48,384]{3,2,1,0:T(8,128)(2,1)S(1)} %maximum_select_fusion.7), channel_id=1, source_target_pairs={{0,1},{1,0},{2,3},{3,2},{4,5},{5,4},{6,7},{7,6},{8,9},{9,8},{10,11... | collective-permute-start | bytes 1327112 | tf_op jit(solution)/shard_map/ppermute | solution.py:570
  50.0 39.9 %collective-permute-start.13 = (bf16[2,4,48,384]{3,2,1,0:T(8,128)(2,1)S(1)}, bf16[2,4,48,384]{3,2,1,0:T(8,128)(2,1)S(1)}, u32[]{:S(2)}, u32[]{:S(2)}) collective-permute-start(bf16[2,4,48,384]{3,2,1,0:T(8,128)(2,1)S(1)} %maximum_select_fusion.9), channel_id=1, source_target_pairs={{0,16},{1,17},{2,18},{3,19},{4,20},{5,21},{6,22},{7,23},{8,24},{9,... | collective-permute-start | bytes 884744 | tf_op jit(solution)/shard_map/ppermute | solution.py:570
  50.2 41.0 %collective-permute-start.19 = (bf16[2,4,48,384]{3,2,1,0:T(8,128)(2,1)S(1)}, bf16[2,4,48,384]{3,2,1,0:T(8,128)(2,1)S(1)}, u32[]{:S(2)}, u32[]{:S(2)}) collective-permute-start(bf16[2,4,48,384]{3,2,1,0:T(8,128)(2,1)S(1)} %maximum_select_fusion.10), channel_id=1, source_target_pairs={{0,16},{1,17},{2,18},{3,19},{4,20},{5,21},{6,22},{7,23},{8,24},{9,... | collective-permute-start | bytes 884744 | tf_op jit(solution)/shard_map/ppermute | solution.py:570
  88.9 32.1 %collective-permute-start.10 = (bf16[2,4,3,48,384]{4,3,2,1,0:T(8,128)(2,1)S(1)}, bf16[2,4,3,48,384]{4,3,2,1,0:T(8,128)(2,1)}, u32[]{:S(2)}, u32[]{:S(2)}) collective-permute-start(bf16[2,4,3,48,384]{4,3,2,1,0:T(8,128)(2,1)S(1)} %pad_maximum_fusion.3.rest_0_), channel_id=1, source_target_pairs={{0,4},{1,5},{2,6},{3,7},{4,0},{5,1},{6,2},{7,3},{8,12},{9,13},{10,... | collective-permute-start | bytes 2654216 | tf_op jit(solution)/shard_map/ppermute | solution.py:570
  90.1 30.3 %collective-permute-start.14 = (bf16[4,4,48,384]{3,2,1,0:T(8,128)(2,1)S(1)}, bf16[4,4,48,384]{3,2,1,0:T(8,128)(2,1)S(1)}, u32[]{:S(2)}, u32[]{:S(2)}) collective-permute-start(bf16[4,4,48,384]{3,2,1,0:T(8,128)(2,1)S(1)} %maximum_select_fusion.3), channel_id=1, source_target_pairs={{0,4},{1,5},{2,6},{3,7},{4,0},{5,1},{6,2},{7,3},{8,12},{9,13},{10,... | collective-permute-start | bytes 1769480 | tf_op jit(solution)/shard_map/ppermute | solution.py:570
  91.1 33.4 %collective-permute-start.9 = (bf16[2,4,3,48,384]{4,3,2,1,0:T(8,128)(2,1)S(1)}, bf16[2,4,3,48,384]{4,3,2,1,0:T(8,128)(2,1)S(1)}, u32[]{:S(2)}, u32[]{:S(2)}) collective-permute-start(bf16[2,4,3,48,384]{4,3,2,1,0:T(8,128)(2,1)S(1)} %pad_maximum_fusion.3.rest_0_), channel_id=1, source_target_pairs={{0,2},{1,3},{2,0},{3,1},{4,6},{5,7},{6,4},{7,5},{8,10},{9,11},{10,... | collective-permute-start | bytes 2654216 | tf_op jit(solution)/shard_map/ppermute | solution.py:570
  91.3 31.1 %collective-permute-start.20 = (bf16[4,4,48,384]{3,2,1,0:T(8,128)(2,1)S(1)}, bf16[4,4,48,384]{3,2,1,0:T(8,128)(2,1)S(1)}, u32[]{:S(2)}, u32[]{:S(2)}) collective-permute-start(bf16[4,4,48,384]{3,2,1,0:T(8,128)(2,1)S(1)} %maximum_select_fusion.5), channel_id=1, source_target_pairs={{0,1},{1,0},{2,3},{3,2},{4,5},{5,4},{6,7},{7,6},{8,9},{9,8},{10,11... | collective-permute-start | bytes 1769480 | tf_op jit(solution)/shard_map/ppermute | solution.py:570
  120.4 33.5 %collective-permute-start.3 = (bf16[2,4,5,48,384]{4,3,2,1,0:T(8,128)(2,1)S(1)}, bf16[2,4,5,48,384]{4,3,2,1,0:T(8,128)(2,1)}, u32[]{:S(2)}, u32[]{:S(2)}) collective-permute-start(bf16[2,4,5,48,384]{4,3,2,1,0:T(8,128)(2,1)S(1)} %pad_maximum_fusion.rest_0_.rest_4_), channel_id=1, source_target_pairs={{0,2},{1,3},{2,0},{3,1},{4,6},{5,7},{6,4},{7,5},{8,10},{9,11},{10,... | collective-permute-start | bytes 4423688 | tf_op jit(solution)/shard_map/ppermute | solution.py:570
  120.4 34.0 %collective-permute-start.5 = (bf16[2,4,5,48,384]{4,3,2,1,0:T(8,128)(2,1)S(1)}, bf16[2,4,5,48,384]{4,3,2,1,0:T(8,128)(2,1)}, u32[]{:S(2)}, u32[]{:S(2)}) collective-permute-start(bf16[2,4,5,48,384]{4,3,2,1,0:T(8,128)(2,1)S(1)} %collective-permute-done.4.rest_2_.rest_6_), channel_id=1, source_target_pairs={{0,2},{1,3},{2,0},{3,1},{4,6},{5,7},{6,4},{7,5},{8,10},{9,11},{10,... | collective-permute-start | bytes 4423688 | tf_op jit(solution)/shard_map/ppermute | solution.py:570
  121.0 15.5 %collective-permute-start.11 = (bf16[2,4,3,48,384]{4,3,2,1,0:T(8,128)(2,1)}, bf16[2,4,3,48,384]{4,3,2,1,0:T(8,128)(2,1)}, u32[]{:S(2)}, u32[]{:S(2)}) collective-permute-start(bf16[2,4,3,48,384]{4,3,2,1,0:T(8,128)(2,1)} %collective-permute-done.10.rest_2_), channel_id=1, source_target_pairs={{0,2},{1,3},{2,0},{3,1},{4,6},{5,7},{6,4},{7,5},{8,10},{9,11},{10,... | collective-permute-start | bytes 2654216 | tf_op jit(solution)/shard_map/ppermute | solution.py:570
  122.4 28.7 %collective-permute-start.16 = (bf16[2,4,4,48,384]{4,3,2,1,0:T(8,128)(2,1)}, bf16[2,4,4,48,384]{4,3,2,1,0:T(8,128)(2,1)}, u32[]{:S(2)}, u32[]{:S(2)}) collective-permute-start(bf16[2,4,4,48,384]{4,3,2,1,0:T(8,128)(2,1)} %pad_maximum_fusion.1.rest_4_), channel_id=1, source_target_pairs={{0,1},{1,0},{2,3},{3,2},{4,5},{5,4},{6,7},{7,6},{8,9},{9,8},{10,11... | collective-permute-start | bytes 3538952 | tf_op jit(solution)/shard_map/ppermute | solution.py:570
  125.5 28.4 %collective-permute-start.22 = (bf16[2,4,4,48,384]{4,3,2,1,0:T(8,128)(2,1)}, bf16[2,4,4,48,384]{4,3,2,1,0:T(8,128)(2,1)}, u32[]{:S(2)}, u32[]{:S(2)}) collective-permute-start(bf16[2,4,4,48,384]{4,3,2,1,0:T(8,128)(2,1)} %pad_maximum_fusion.2.rest_0_), channel_id=1, source_target_pairs={{0,4},{1,5},{2,6},{3,7},{4,0},{5,1},{6,2},{7,3},{8,12},{9,13},{10,... | collective-permute-start | bytes 3538952 | tf_op jit(solution)/shard_map/ppermute | solution.py:570
  136.5 63.7 %collective-permute-start.15 = (bf16[2,4,4,48,384]{4,3,2,1,0:T(8,128)(2,1)}, bf16[2,4,4,48,384]{4,3,2,1,0:T(8,128)(2,1)S(1)}, u32[]{:S(2)}, u32[]{:S(2)}) collective-permute-start(bf16[2,4,4,48,384]{4,3,2,1,0:T(8,128)(2,1)} %pad_maximum_fusion.1.rest_4_), channel_id=1, source_target_pairs={{0,2},{1,3},{2,0},{3,1},{4,6},{5,7},{6,4},{7,5},{8,10},{9,11},{10,... | collective-permute-start | bytes 3538952 | tf_op jit(solution)/shard_map/ppermute | solution.py:570
  151.1 68.5 %collective-permute-start.21 = (bf16[2,4,4,48,384]{4,3,2,1,0:T(8,128)(2,1)}, bf16[2,4,4,48,384]{4,3,2,1,0:T(8,128)(2,1)S(1)}, u32[]{:S(2)}, u32[]{:S(2)}) collective-permute-start(bf16[2,4,4,48,384]{4,3,2,1,0:T(8,128)(2,1)} %pad_maximum_fusion.2.rest_0_), channel_id=1, source_target_pairs={{0,2},{1,3},{2,0},{3,1},{4,6},{5,7},{6,4},{7,5},{8,10},{9,11},{10,... | collective-permute-start | bytes 3538952 | tf_op jit(solution)/shard_map/ppermute | solution.py:570
  153.9 46.3 %collective-permute-start.17 = (bf16[2,4,4,48,384]{4,3,2,1,0:T(8,128)(2,1)}, bf16[2,4,4,48,384]{4,3,2,1,0:T(8,128)(2,1)S(1)}, u32[]{:S(2)}, u32[]{:S(2)}) collective-permute-start(bf16[2,4,4,48,384]{4,3,2,1,0:T(8,128)(2,1)} %collective-permute-done.16.rest_6_), channel_id=1, source_target_pairs={{0,2},{1,3},{2,0},{3,1},{4,6},{5,7},{6,4},{7,5},{8,10},{9,11},{10,... | collective-permute-start | bytes 3538952 | tf_op jit(solution)/shard_map/ppermute | solution.py:570
  153.9 65.7 %collective-permute-start.23 = (bf16[2,4,4,48,384]{4,3,2,1,0:T(8,128)(2,1)}, bf16[2,4,4,48,384]{4,3,2,1,0:T(8,128)(2,1)S(1)}, u32[]{:S(2)}, u32[]{:S(2)}) collective-permute-start(bf16[2,4,4,48,384]{4,3,2,1,0:T(8,128)(2,1)} %collective-permute-done.22.rest_2_), channel_id=1, source_target_pairs={{0,2},{1,3},{2,0},{3,1},{4,6},{5,7},{6,4},{7,5},{8,10},{9,11},{10,... | collective-permute-start | bytes 3538952 | tf_op jit(solution)/shard_map/ppermute | solution.py:570
  291.7 27.8 %collective-permute-start.29 = (bf16[4,2,2,5,48,384]{5,4,3,2,1,0:T(8,128)(2,1)}, bf16[4,2,2,5,48,384]{5,4,3,2,1,0:T(8,128)(2,1)}, u32[]{:S(2)}, u32[]{:S(2)}) collective-permute-start(bf16[4,2,2,5,48,384]{5,4,3,2,1,0:T(8,128)(2,1)} %get-tuple-element.108), channel_id=1, source_target_pairs={{0,2},{1,3},{2,0},{3,1},{4,6},{5,7},{6,4},{7,5},{8,10},{9,11},{10,... | collective-permute-start | bytes 8847368 | tf_op jit(solution)/shard_map/ppermute | solution.py:570
  291.7 36.8 %collective-permute-start.39 = (bf16[4,2,2,4,48,384]{5,4,3,2,1,0:T(8,128)(2,1)}, bf16[4,2,2,4,48,384]{5,4,3,2,1,0:T(8,128)(2,1)}, u32[]{:S(2)}, u32[]{:S(2)}) collective-permute-start(bf16[4,2,2,4,48,384]{5,4,3,2,1,0:T(8,128)(2,1)} %get-tuple-element.112), channel_id=1, source_target_pairs={{0,2},{1,3},{2,0},{3,1},{4,6},{5,7},{6,4},{7,5},{8,10},{9,11},{10,... | collective-permute-start | bytes 7077896 | tf_op jit(solution)/shard_map/ppermute | solution.py:570
  292.2 39.1 %collective-permute-start.34 = (bf16[4,2,2,4,48,384]{5,4,3,2,1,0:T(8,128)(2,1)}, bf16[4,2,2,4,48,384]{5,4,3,2,1,0:T(8,128)(2,1)}, u32[]{:S(2)}, u32[]{:S(2)}) collective-permute-start(bf16[4,2,2,4,48,384]{5,4,3,2,1,0:T(8,128)(2,1)} %get-tuple-element.110), channel_id=1, source_target_pairs={{0,2},{1,3},{2,0},{3,1},{4,6},{5,7},{6,4},{7,5},{8,10},{9,11},{10,... | collective-permute-start | bytes 7077896 | tf_op jit(solution)/shard_map/ppermute | solution.py:570
  312.7 4.2 collective-permute-start.24
  319.4 24.6 %collective-permute-start.25 = (bf16[4,2,1,3,48,384]{5,4,3,2,1,0:T(8,128)(2,1)}, bf16[4,2,1,3,48,384]{5,4,3,2,1,0:T(8,128)(2,1)}, u32[]{:S(2)}, u32[]{:S(2)}) collective-permute-start(bf16[4,2,1,3,48,384]{5,4,3,2,1,0:T(8,128)(2,1)} %add_convert_fusion.3), channel_id=1, source_target_pairs={{0,1},{1,0},{2,3},{3,2},{4,5},{5,4},{6,7},{7,6},{8,9},{9,8},{10,11... | collective-permute-start | bytes 2654216 | tf_op jit(solution)/shard_map/ppermute | solution.py:570
  322.6 73.7 %collective-permute-start.30 = (bf16[4,1,2,5,48,384]{5,4,3,2,1,0:T(8,128)(2,1)}, bf16[4,1,2,5,48,384]{5,4,3,2,1,0:T(8,128)(2,1)}, u32[]{:S(2)}, u32[]{:S(2)}) collective-permute-start(bf16[4,1,2,5,48,384]{5,4,3,2,1,0:T(8,128)(2,1)} %add_convert_fusion), channel_id=1, source_target_pairs={{0,4},{1,5},{2,6},{3,7},{4,0},{5,1},{6,2},{7,3},{8,12},{9,13},{10,... | collective-permute-start | bytes 4423688 | tf_op jit(solution)/shard_map/ppermute | solution.py:570
  331.3 55.9 %collective-permute-start.40 = (bf16[4,1,2,4,48,384]{5,4,3,2,1,0:T(8,128)(2,1)}, bf16[4,1,2,4,48,384]{5,4,3,2,1,0:T(8,128)(2,1)}, u32[]{:S(2)}, u32[]{:S(2)}) collective-permute-start(bf16[4,1,2,4,48,384]{5,4,3,2,1,0:T(8,128)(2,1)} %add_convert_fusion.1), channel_id=1, source_target_pairs={{0,4},{1,5},{2,6},{3,7},{4,0},{5,1},{6,2},{7,3},{8,12},{9,13},{10,... | collective-permute-start | bytes 3538952 | tf_op jit(solution)/shard_map/ppermute | solution.py:570
  334.0 57.8 %collective-permute-start.35 = (bf16[4,2,1,4,48,384]{5,4,3,2,1,0:T(8,128)(2,1)}, bf16[4,2,1,4,48,384]{5,4,3,2,1,0:T(8,128)(2,1)}, u32[]{:S(2)}, u32[]{:S(2)}) collective-permute-start(bf16[4,2,1,4,48,384]{5,4,3,2,1,0:T(8,128)(2,1)} %add_convert_fusion.2), channel_id=1, source_target_pairs={{0,1},{1,0},{2,3},{3,2},{4,5},{5,4},{6,7},{7,6},{8,9},{9,8},{10,11... | collective-permute-start | bytes 3538952 | tf_op jit(solution)/shard_map/ppermute | solution.py:570
  346.3 52.5 %collective-permute-start.26 = (bf16[4,1,1,3,48,384]{5,4,3,2,1,0:T(8,128)(2,1)}, bf16[4,1,1,3,48,384]{5,4,3,2,1,0:T(8,128)(2,1)}, u32[]{:S(2)}, u32[]{:S(2)}) collective-permute-start(bf16[4,1,1,3,48,384]{5,4,3,2,1,0:T(8,128)(2,1)} %add_convert_fusion.7), channel_id=1, source_target_pairs={{0,4},{1,5},{2,6},{3,7},{4,0},{5,1},{6,2},{7,3},{8,12},{9,13},{10,... | collective-permute-start | bytes 1327112 | tf_op jit(solution)/shard_map/ppermute | solution.py:570
  389.7 32.2 %collective-permute-start.41 = (bf16[4,1,1,4,48,384]{5,4,3,2,1,0:T(8,128)(2,1)}, bf16[4,1,1,4,48,384]{5,4,3,2,1,0:T(8,128)(2,1)}, u32[]{:S(2)}, u32[]{:S(2)}) collective-permute-start(bf16[4,1,1,4,48,384]{5,4,3,2,1,0:T(8,128)(2,1)} %add_convert_fusion.5), channel_id=1, source_target_pairs={{0,1},{1,0},{2,3},{3,2},{4,5},{5,4},{6,7},{7,6},{8,9},{9,8},{10,11... | collective-permute-start | bytes 1769480 | tf_op jit(solution)/shard_map/ppermute | solution.py:570
  394.2 32.7 %collective-permute-start.36 = (bf16[4,1,1,4,48,384]{5,4,3,2,1,0:T(8,128)(2,1)}, bf16[4,1,1,4,48,384]{5,4,3,2,1,0:T(8,128)(2,1)S(1)}, u32[]{:S(2)}, u32[]{:S(2)}) collective-permute-start(bf16[4,1,1,4,48,384]{5,4,3,2,1,0:T(8,128)(2,1)} %add_convert_fusion.6), channel_id=1, source_target_pairs={{0,4},{1,5},{2,6},{3,7},{4,0},{5,1},{6,2},{7,3},{8,12},{9,13},{10,... | collective-permute-start | bytes 1769480 | tf_op jit(solution)/shard_map/ppermute | solution.py:570
  398.8 30.4 %collective-permute-start.31 = (bf16[4,1,1,5,48,384]{5,4,3,2,1,0:T(8,128)(2,1)}, bf16[4,1,1,5,48,384]{5,4,3,2,1,0:T(8,128)(2,1)}, u32[]{:S(2)}, u32[]{:S(2)}) collective-permute-start(bf16[4,1,1,5,48,384]{5,4,3,2,1,0:T(8,128)(2,1)} %add_convert_fusion.4), channel_id=1, source_target_pairs={{0,1},{1,0},{2,3},{3,2},{4,5},{5,4},{6,7},{7,6},{8,9},{9,8},{10,11... | collective-permute-start | bytes 2211848 | tf_op jit(solution)/shard_map/ppermute | solution.py:570
  400.8 15.7 %collective-permute-start.27 = (bf16[2,1,1,3,48,384]{5,4,3,2,1,0:T(8,128)(2,1)}, bf16[2,1,1,3,48,384]{5,4,3,2,1,0:T(8,128)(2,1)}, u32[]{:S(2)}, u32[]{:S(2)}) collective-permute-start(bf16[2,1,1,3,48,384]{5,4,3,2,1,0:T(8,128)(2,1)} %add_convert_fusion.11), channel_id=1, source_target_pairs={{0,16},{1,17},{2,18},{3,19},{4,20},{5,21},{6,22},{7,23},{8,24},{9,... | collective-permute-start | bytes 663560 | tf_op jit(solution)/shard_map/ppermute | solution.py:570
  417.8 16.5 %collective-permute-start.28 = (bf16[1,1,1,3,48,384]{5,4,3,2,1,0:T(8,128)(2,1)S(1)}, bf16[1,1,1,3,48,384]{5,4,3,2,1,0:T(8,128)(2,1)S(1)}, u32[]{:S(2)}, u32[]{:S(2)}) collective-permute-start(bf16[1,1,1,3,48,384]{5,4,3,2,1,0:T(8,128)(2,1)S(1)} %add_convert_fusion.15), channel_id=1, source_target_pairs={{0,8},{1,9},{2,10},{3,11},{4,12},{5,13},{6,14},{7,15},{8,0},{9,1},... | collective-permute-start | bytes 331784 | tf_op jit(solution)/shard_map/ppermute | solution.py:570
  424.0 29.0 %collective-permute-start.42 = (bf16[2,1,1,4,48,384]{5,4,3,2,1,0:T(8,128)(2,1)}, bf16[2,1,1,4,48,384]{5,4,3,2,1,0:T(8,128)(2,1)}, u32[]{:S(2)}, u32[]{:S(2)}) collective-permute-start(bf16[2,1,1,4,48,384]{5,4,3,2,1,0:T(8,128)(2,1)} %add_convert_fusion.9), channel_id=1, source_target_pairs={{0,16},{1,17},{2,18},{3,19},{4,20},{5,21},{6,22},{7,23},{8,24},{9,... | collective-permute-start | bytes 884744 | tf_op jit(solution)/shard_map/ppermute | solution.py:570
  429.1 30.3 %collective-permute-start.37 = (bf16[2,1,1,4,48,384]{5,4,3,2,1,0:T(8,128)(2,1)}, bf16[2,1,1,4,48,384]{5,4,3,2,1,0:T(8,128)(2,1)}, u32[]{:S(2)}, u32[]{:S(2)}) collective-permute-start(bf16[2,1,1,4,48,384]{5,4,3,2,1,0:T(8,128)(2,1)} %add_convert_fusion.10), channel_id=1, source_target_pairs={{0,16},{1,17},{2,18},{3,19},{4,20},{5,21},{6,22},{7,23},{8,24},{9,... | collective-permute-start | bytes 884744 | tf_op jit(solution)/shard_map/ppermute | solution.py:570
  431.3 34.8 %collective-permute-start.32 = (bf16[2,1,1,5,48,384]{5,4,3,2,1,0:T(8,128)(2,1)}, bf16[2,1,1,5,48,384]{5,4,3,2,1,0:T(8,128)(2,1)}, u32[]{:S(2)}, u32[]{:S(2)}) collective-permute-start(bf16[2,1,1,5,48,384]{5,4,3,2,1,0:T(8,128)(2,1)} %add_convert_fusion.8), channel_id=1, source_target_pairs={{0,16},{1,17},{2,18},{3,19},{4,20},{5,21},{6,22},{7,23},{8,24},{9,... | collective-permute-start | bytes 1105928 | tf_op jit(solution)/shard_map/ppermute | solution.py:570
  454.3 14.8 %collective-permute-start.43 = (bf16[1,1,1,4,48,384]{5,4,3,2,1,0:T(8,128)(2,1)S(1)}, bf16[1,1,1,4,48,384]{5,4,3,2,1,0:T(8,128)(2,1)S(1)}, u32[]{:S(2)}, u32[]{:S(2)}) collective-permute-start(bf16[1,1,1,4,48,384]{5,4,3,2,1,0:T(8,128)(2,1)S(1)} %add_convert_fusion.13), channel_id=1, source_target_pairs={{0,8},{1,9},{2,10},{3,11},{4,12},{5,13},{6,14},{7,15},{8,0},{9,1},... | collective-permute-start | bytes 442376 | tf_op jit(solution)/shard_map/ppermute | solution.py:570
  460.7 11.7 %collective-permute-start.38 = (bf16[1,1,1,4,48,384]{5,4,3,2,1,0:T(8,128)(2,1)S(1)}, bf16[1,1,1,4,48,384]{5,4,3,2,1,0:T(8,128)(2,1)}, u32[]{:S(2)}, u32[]{:S(2)}) collective-permute-start(bf16[1,1,1,4,48,384]{5,4,3,2,1,0:T(8,128)(2,1)S(1)} %add_convert_fusion.14), channel_id=1, source_target_pairs={{0,8},{1,9},{2,10},{3,11},{4,12},{5,13},{6,14},{7,15},{8,0},{9,1},... | collective-permute-start | bytes 442376 | tf_op jit(solution)/shard_map/ppermute | solution.py:570
  467.4 8.8 %collective-permute-start.33 = (bf16[1,1,1,5,48,384]{5,4,3,2,1,0:T(8,128)(2,1)S(1)}, bf16[1,1,1,5,48,384]{5,4,3,2,1,0:T(8,128)(2,1)}, u32[]{:S(2)}, u32[]{:S(2)}) collective-permute-start(bf16[1,1,1,5,48,384]{5,4,3,2,1,0:T(8,128)(2,1)S(1)} %add_convert_fusion.12), channel_id=1, source_target_pairs={{0,8},{1,9},{2,10},{3,11},{4,12},{5,13},{6,14},{7,15},{8,0},{9,1},... | collective-permute-start | bytes 552968 | tf_op jit(solution)/shard_map/ppermute | solution.py:570
  478.3 50.4 %copy-start.13 = (f32[48,384]{1,0:T(8,128)}, f32[48,384]{1,0:T(8,128)S(1)}, u32[]{:S(2)}) copy-start(f32[48,384]{1,0:T(8,128)S(1)} %get-tuple-element.184) | copy-start | bytes 221188
  478.3 51.9 %copy-start.14 = (f32[48,384]{1,0:T(8,128)}, f32[48,384]{1,0:T(8,128)S(1)}, u32[]{:S(2)}) copy-start(f32[48,384]{1,0:T(8,128)S(1)} %get-tuple-element.173) | copy-start | bytes 221188
  478.3 51.9 %copy-start.15 = (f32[48,384]{1,0:T(8,128)}, f32[48,384]{1,0:T(8,128)S(1)}, u32[]{:S(2)}) copy-start(f32[48,384]{1,0:T(8,128)S(1)} %get-tuple-element.180) | copy-start | bytes 221188
  484.3 9.3 %collective-permute-start.44 = (f32[3175]{0:T(1024)S(1)}, f32[3175]{0:T(1024)S(1)}, u32[]{:S(2)}, u32[]{:S(2)}) collective-permute-start(f32[3175]{0:T(1024)S(1)} %concatenate.226), channel_id=1, source_target_pairs={{0,1},{1,0},{2,3},{3,2},{4,5},{5,4},{6,7},{7,6},{8,9},{9,8},{10,11... | collective-permute-start | bytes 38108 | tf_op jit(solution)/shard_map/ppermute | solution.py:570
  495.0 11.7 %collective-permute-start.45 = (f32[7687]{0:T(1024)}, f32[7687]{0:T(1024)S(1)}, u32[]{:S(2)}, u32[]{:S(2)}) collective-permute-start(f32[7687]{0:T(1024)} %slice_dynamic-update-slice_fusion), channel_id=1, source_target_pairs={{0,2},{1,3},{2,0},{3,1},{4,6},{5,7},{6,4},{7,5},{8,10},{9,11},{10,... | collective-permute-start | bytes 92252 | tf_op jit(solution)/shard_map/ppermute | solution.py:570
  506.7 23.5 %copy-start.9 = (f32[3,6,8,384]{3,2,0,1:T(8,128)}, f32[3,6,8,384]{3,2,0,1:T(8,128)S(1)}, u32[]{:S(2)}) copy-start(f32[3,6,8,384]{3,2,0,1:T(8,128)S(1)} %copy.64) | copy-start | bytes 663556
  506.7 24.2 %copy-start.5 = (f32[4,6,8,384]{3,2,0,1:T(8,128)}, f32[4,6,8,384]{3,2,0,1:T(8,128)S(1)}, u32[]{:S(2)}) copy-start(f32[4,6,8,384]{3,2,0,1:T(8,128)S(1)} %copy.66) | copy-start | bytes 884740
  506.8 4.0 collective-permute-start.46
  508.2 22.7 %copy-start.10 = (f32[2,6,8,384]{3,2,0,1:T(8,128)}, f32[2,6,8,384]{3,2,0,1:T(8,128)S(1)}, u32[]{:S(2)}) copy-start(f32[2,6,8,384]{3,2,0,1:T(8,128)S(1)} %copy.65) | copy-start | bytes 442372
  510.7 3.9 collective-permute-start.47
  510.8 20.1 %copy-start.36 = (f32[48]{0:T(128)}, f32[48]{0:T(128)S(1)}, u32[]{:S(2)}) copy-start(f32[48]{0:T(128)S(1)} %get-tuple-element.205) | copy-start | bytes 580
  510.8 20.1 %copy-start.37 = (f32[48]{0:T(128)}, f32[48]{0:T(128)S(1)}, u32[]{:S(2)}) copy-start(f32[48]{0:T(128)S(1)} %get-tuple-element.206) | copy-start | bytes 580
  510.9 20.1 %copy-start.38 = (f32[48]{0:T(128)}, f32[48]{0:T(128)S(1)}, u32[]{:S(2)}) copy-start(f32[48]{0:T(128)S(1)} %get-tuple-element.207) | copy-start | bytes 580
  510.9 20.1 %copy-start.39 = (f32[48]{0:T(128)}, f32[48]{0:T(128)S(1)}, u32[]{:S(2)}) copy-start(f32[48]{0:T(128)S(1)} %get-tuple-element.208) | copy-start | bytes 580
  514.7 4.8 collective-permute-start.48
  (30 other events, 256.1 us)
